TPU v7x, 32 devices: a whole 2x2x4 slice. The times are simulated.
32 devices in a mesh: head: 2 (over y), frame: 16 (over z, x, core).
Axes of the slice: x: 2, y: 2, z: 4, core: 2. Of those that a mesh axis runs over, the one named last changes fastest.
Arguments:
- queries: bfloat16 [16384, 16, 128], P(('frame', 'head')), may hold values from -30 to 30
- keys: bfloat16 [16384, 16, 128], P(('frame', 'head')), may hold values from -4 to 4
- values: bfloat16 [16384, 16, 128], P(('frame', 'head')), may hold values from -24 to 24
- block_mask: int32 [16, 16, 16], replicated, may hold values from 0 to 1, as said below
- strides: int32 [16], replicated, may hold values from 1 to 16, as said below
- offsets: int32 [16], replicated, may hold values from 0 to 15
Outputs:
- attended: bfloat16 [16384, 16, 128], P(('frame', 'head'))
Inputs may be any that keep to these rules, and one draw needn't show every extreme that they name: Every diagonal entry block_mask[i, b, b] is 1. strides[0] is 1, strides[1] is 4, 8 or 16, and every later entry is 8 or 16.
All inputs are finite; a program needn't handle non-finite values.
Results may differ from a plain program's by a relative error of at most 0.0043.
Values may be sent and summed in bfloat16 or wider, within the bound.
A program may use at most 128 MiB of HBM per device.

v0:
```python
import jax
import jax.numpy as jnp
from jax import lax
from jax.sharding import PartitionSpec as P

masked_score = -1e30


def passed_along(block, axis, distance):
    devices = range(lax.axis_size(axis))
    route = [(i - distance, i) for i in devices if i - distance in devices]
    return lax.ppermute(block, axis, route)


def group_terms(query_blocks, key_rows, value_rows, keep_mask, score_scale):
    scores = (
        jnp.einsum("qahd,gnhd->hqagn", query_blocks, key_rows, preferred_element_type=jnp.float32)
        * score_scale
    )
    allowed = keep_mask[None, :, None, :, :]
    scores = jnp.where(allowed, scores, masked_score)
    group_tops = jnp.max(scores, axis=4)
    weights = jnp.where(allowed, jnp.exp(scores - group_tops[..., None]), 0.0)
    group_totals = jnp.sum(weights, axis=4)
    group_sums = jnp.einsum(
        "hqagn,gnhd->hqagd",
        weights.astype(jnp.bfloat16),
        value_rows,
        preferred_element_type=jnp.float32,
    )
    return (group_tops, group_totals, group_sums)


def absorb(carry_state, group_tops, group_totals, group_sums):
    running_top, running_total, running_sum = carry_state
    new_top = jnp.maximum(running_top, jnp.max(group_tops, axis=3))
    shrink = jnp.exp(running_top - new_top)
    factors = jnp.exp(group_tops - new_top[..., None])
    running_total = running_total * shrink + jnp.sum(factors * group_totals, axis=3)
    running_sum = running_sum * shrink[..., None] + jnp.sum(factors[..., None] * group_sums, axis=3)
    return (new_top, running_total, running_sum)


def pick_blocks(key_blocks, value_blocks, offsets, source_frame, spacing, block_count):
    first_block = (spacing - offsets[source_frame] % spacing) % spacing
    chosen = first_block + spacing * jnp.arange(block_count, dtype=jnp.int32)
    return jnp.stack([jnp.take(key_blocks, chosen, axis=0), jnp.take(value_blocks, chosen, axis=0)])


def local(queries, keys, values, block_mask, strides, offsets):
    local_queries, local_keys, local_values = (
        lax.all_to_all(queries, "head", split_axis=1, concat_axis=0, tiled=True),
        lax.all_to_all(keys, "head", split_axis=1, concat_axis=0, tiled=True),
        lax.all_to_all(values, "head", split_axis=1, concat_axis=0, tiled=True),
    )
    frame_rows, heads_here, head_dim = local_queries.shape
    frame_blocks = block_mask.shape[1]
    block_rows = frame_rows // frame_blocks
    score_scale = head_dim ** (-0.5)
    frame_index = lax.axis_index("frame")
    frame_total = lax.axis_size("frame")
    query_blocks = local_queries.reshape(frame_blocks, block_rows, heads_here, head_dim)
    key_blocks = local_keys.reshape(frame_blocks, block_rows, heads_here, head_dim)
    value_blocks = local_values.reshape(frame_blocks, block_rows, heads_here, head_dim)
    own_mask = lax.dynamic_index_in_dim(block_mask, frame_index, 0, keepdims=False) == 1
    carry_state = (
        jnp.full((heads_here, frame_blocks, block_rows), masked_score, jnp.float32),
        jnp.zeros((heads_here, frame_blocks, block_rows), jnp.float32),
        jnp.zeros((heads_here, frame_blocks, block_rows, head_dim), jnp.float32),
    )
    half_blocks = frame_blocks // 2
    whole_keys = local_keys.reshape(1, frame_rows, heads_here, head_dim)
    whole_values = local_values.reshape(1, frame_rows, heads_here, head_dim)
    results = []
    for first_block in (0, half_blocks):
        keep_mask = jnp.repeat(
            own_mask[first_block : first_block + half_blocks], block_rows, axis=1
        )[:, None, :]
        results.append(
            group_terms(
                query_blocks[first_block : first_block + half_blocks],
                whole_keys,
                whole_values,
                keep_mask,
                score_scale,
            )
        )
    carry_state = absorb(
        carry_state,
        jnp.concatenate([entry[0] for entry in results], axis=1),
        jnp.concatenate([entry[1] for entry in results], axis=1),
        jnp.concatenate([entry[2] for entry in results], axis=1),
    )

    def attend_near(state_now, arrived, source_frame, spacing, block_count, distance):
        valid = (source_frame >= 0) & (source_frame < frame_total)
        clipped = jnp.clip(source_frame, 0, frame_total - 1)
        chosen = (spacing - offsets[clipped] % spacing) % spacing + spacing * jnp.arange(
            block_count, dtype=jnp.int32
        )
        phase_ok = (chosen + offsets[clipped]) % strides[distance] == 0
        kept = valid & own_mask[:, chosen] & phase_ok[None, :]
        keep_mask = jnp.repeat(kept, block_rows, axis=1)[:, None, :]
        near_keys = arrived[0].reshape(1, block_count * block_rows, heads_here, head_dim)
        near_values = arrived[1].reshape(1, block_count * block_rows, heads_here, head_dim)
        return absorb(
            state_now, *group_terms(query_blocks, near_keys, near_values, keep_mask, score_scale)
        )

    wide_spacing = frame_blocks // 4
    narrow_spacing = frame_blocks // 2
    packed = pick_blocks(key_blocks, value_blocks, offsets, frame_index, wide_spacing, 4)
    for direction in (1, -1):
        arrived = passed_along(packed, "frame", direction)
        source_frame = frame_index - direction
        carry_state = attend_near(carry_state, arrived, source_frame, wide_spacing, 4, 1)
        clipped = jnp.clip(source_frame, 0, frame_total - 1)
        narrow_first = (narrow_spacing - offsets[clipped] % narrow_spacing) % narrow_spacing
        parity = (narrow_first >= wide_spacing).astype(jnp.int32)
        paired = arrived.reshape(2, 2, 2, block_rows, heads_here, head_dim)
        passed = lax.dynamic_index_in_dim(paired, parity, 2, keepdims=False)
        for relay_step in (2, 3):
            passed = passed_along(passed, "frame", direction)
            carry_state = attend_near(
                carry_state,
                passed,
                frame_index - direction * relay_step,
                narrow_spacing,
                2,
                relay_step,
            )
    anchor_block = (frame_blocks - offsets[frame_index] % frame_blocks) % frame_blocks
    anchor_pair = jnp.stack([key_blocks[anchor_block], value_blocks[anchor_block]])[None]
    gathered = lax.all_gather(anchor_pair, "frame", axis=0, tiled=True)
    piece_frames = gathered.shape[0]
    group_width = 4
    grouped = gathered.reshape(
        piece_frames // group_width, group_width, 2, block_rows, heads_here, head_dim
    )

    def one_group(state_inner, entry):
        group_blocks, group_number = entry
        sources = 0 + group_number * group_width + jnp.arange(group_width, dtype=jnp.int32)
        distances = jnp.abs(frame_index - sources)
        spots = (frame_blocks - offsets[sources] % frame_blocks) % frame_blocks
        phase_ok = (spots + offsets[sources]) % strides[distances] == 0
        kept = (distances >= 4)[None, :] & own_mask[:, spots] & phase_ok[None, :]
        keep_mask = jnp.repeat(kept, block_rows, axis=1).reshape(
            frame_blocks, group_width, block_rows
        )
        terms = group_terms(
            query_blocks, group_blocks[:, 0], group_blocks[:, 1], keep_mask, score_scale
        )
        return (absorb(state_inner, *terms), None)

    numbers = jnp.arange(piece_frames // group_width, dtype=jnp.int32)
    state_out, unused = lax.scan(one_group, carry_state, (grouped, numbers))
    carry_state = state_out
    running_top, running_total, running_sum = carry_state
    output = (running_sum / running_total[..., None]).astype(jnp.bfloat16)
    output = jnp.transpose(output, (1, 2, 0, 3)).reshape(frame_rows, heads_here, head_dim)
    return lax.all_to_all(output, "head", split_axis=0, concat_axis=1, tiled=True)


def solution(mesh):
    placed = (
        P(("frame", "head"), None, None),
        P(("frame", "head"), None, None),
        P(("frame", "head"), None, None),
        P(),
        P(),
        P(),
    )
    return jax.shard_map(
        local,
        mesh=mesh,
        in_specs=placed,
        out_specs=P(("frame", "head"), None, None),
        check_vma=False,
    )
```

profile of v0, /device:TPU:3, one launch (start us, length us, event | category | flops | bytes accessed | tf_op | source)
XLA Modules:
  0.0 461.6 jit_solution(16185744266586951488)
XLA Ops:
  41.9 4.8 %all-to-all-start.2 = ((bf16[512,16,128]{2,0,1:T(8,128)(2,1)}), bf16[512,16,128]{2,0,1:T(8,128)(2,1)}, u32[]{:S(2)}, u32[]{:S(2)}) async-start(bf16[512,16,128]{2,0,1:T(8,128)(2,1)} %copy.79), calls=%async_computation.2 | async-start | bytes 4194304 | tf_op jit(solution)/shard_map/all_to_all | solution.py:54
  53.1 18.0 %all-to-all-done.2 = bf16[512,16,128]{2,0,1:T(8,128)(2,1)} async-done(((bf16[512,16,128]{2,0,1:T(8,128)(2,1)}), bf16[512,16,128]{2,0,1:T(8,128)(2,1)}, u32[]{:S(2)}, u32[]{:S(2)}) %all-to-all-start.2) | async-done | bytes 2097184 | tf_op jit(solution)/shard_map/all_to_all | solution.py:54
  71.0 4.8 %all-to-all-start = ((bf16[512,16,128]{2,0,1:T(8,128)(2,1)}), bf16[512,16,128]{2,0,1:T(8,128)(2,1)}, u32[]{:S(2)}, u32[]{:S(2)}) async-start(bf16[512,16,128]{2,0,1:T(8,128)(2,1)} %copy.73), calls=%async_computation | async-start | bytes 4194304 | tf_op jit(solution)/shard_map/all_to_all | solution.py:52
  80.3 4.2 copy.81
  105.6 7.1 %fusion.19 = (f32[8,8,64]{2,1,0:T(8,128)S(1)}, f32[8,8,64,1024]{3,2,1,0:T(8,128)}) fusion(pred[8,1024]{1,0:T(8,128)(4,1)S(1)} %broadcast_in_dim.250, bf16[8,64,8,128]{3,1,0,2:T(8,128)(2,1)S(1)} %bitcast.439, bf16[1024,8,128,1]{2,0,3,1:T(8,128)(2,1)S(1)} %bitcast.434), kind=kOutput, calls=%fused_computation.69 | convolution fusion | flops 1086320640 | bytes 19947520 | tf_op jit(solution)/shard_map/qahd,gnhd->hqagn/dot_general | solution.py:17
  112.7 5.7 %fusion.26 = f32[8,8,64,128]{3,2,1,0:T(8,128)} fusion(bf16[1024,8,128,1]{2,0,3,1:T(8,128)(2,1)S(1)} %bitcast.446, f32[8,8,64,1024]{3,2,1,0:T(8,128)S(1)} %get-tuple-element.264, f32[8,8,64]{2,1,0:T(8,128)S(1)} %get-tuple-element.263, pred[8,1024]{1,0:T(8,128)(4,1)S(1)} %broadcast_in_dim.246), kind=kOutput, calls=%fused_computation.79 | convolution fusion | flops 1094713344 | bytes 20996096 | tf_op jit(solution)/shard_map/hqagn,gnhd->hqagd/dot_general | solution.py:25
  118.4 11.8 %fusion.21 = (f32[8,8,64]{2,1,0:T(8,128)S(1)}, f32[8,8,64]{2,1,0:T(8,128)S(1)}) fusion(f32[8,8,64,1024]{3,2,1,0:T(8,128)S(1)} %get-tuple-element.264, f32[8,8,64]{2,1,0:T(8,128)S(1)} %get-tuple-element.263, pred[8,1024]{1,0:T(8,128)(4,1)S(1)} %broadcast_in_dim.246, f32[8,8,64]{2,1,0:T(8,128)S(1)} %get-tuple-element.261, ...), kind=kLoop, calls=%fused_computation.71 | loop fusion | flops 41934848 | bytes 33636352 | tf_op jit(solution)/shard_map/reduce_sum | solution.py:24
  130.2 9.2 %fusion.24 = f32[8,8,64,128]{3,2,1,0:T(8,128)} fusion(bf16[1024,8,128,1]{2,0,3,1:T(8,128)(2,1)S(1)} %bitcast.447, f32[8,8,64,1024]{3,2,1,0:T(8,128)} %get-tuple-element.262, f32[8,8,64]{2,1,0:T(8,128)S(1)} %get-tuple-element.261, pred[8,1024]{1,0:T(8,128)(4,1)S(1)} %broadcast_in_dim.250), kind=kOutput, calls=%fused_computation.78 | convolution fusion | flops 1094713344 | bytes 20996096 | tf_op jit(solution)/shard_map/hqagn,gnhd->hqagd/dot_general | solution.py:25
  144.1 4.4 collective-permute-start.4
  187.4 4.5 collective-permute-start.2
  194.4 6.7 %collective-permute-done.2 = bf16[2,2,64,8,128]{4,2,1,3,0:T(8,128)(2,1)S(1)} collective-permute-done((bf16[2,2,64,8,128]{4,2,1,3,0:T(8,128)(2,1)S(1)}, bf16[2,2,64,8,128]{4,2,1,3,0:T(8,128)(2,1)S(1)}, u32[]{:S(2)}, u32[]{:S(2)}) %collective-permute-start.2) | collective-permute-done | bytes 524320 | tf_op jit(solution)/shard_map/ppermute | solution.py:12
  212.9 20.5 %fusion.52 = f32[8,16,64,128]{3,2,1,0:T(8,128)} fusion(f32[8,8,64,128]{3,2,1,0:T(8,128)S(1)} %copy-done.8, f32[8,8,64,128]{3,2,1,0:T(8,128)S(1)} %copy-done.7, f32[8,128,16,64]{1,3,2,0:T(8,128)S(1)} %fusion.76, f32[8,128,16,64]{1,3,2,0:T(8,128)S(1)} %fusion.36, f32[8,128,16,64]{1,3,2,0:T(8,128)S(1)} %fusion.78, f32[8,128,16,64]{1,3,2,0:T(8,128)S(1)} %fusion.80, ...), kind=kOutput, calls=%fused_computation.103 | convolution fusion | flops 295698432 | bytes 34310144 | tf_op jit(solution)/shard_map/hqagn,gnhd->hqagd/dot_general | solution.py:25
  233.4 188.2 %while.16 = (s32[]{:T(128)}, f32[8,16,64]{2,1,0:T(8,128)S(1)}, f32[8,16,64]{2,1,0:T(8,128)S(1)}, f32[8,16,64,128]{3,2,1,0:T(8,128)}, s32[]{:T(128)}, /*index=5*/...) while((s32[]{:T(128)}, f32[8,16,64]{2,1,0:T(8,128)S(1)}, ...), condition=%wide.region_22.24_spmd, body=%wide.region_16.23_spmd.sunk | while | flops 1104203264 | bytes 101299536 | solution.py:157
  242.5 12.2 %fusion.225 = (f32[8,16,64,4]{2,1,3,0:T(8,128)S(1)}, f32[8,16,64]{2,1,0:T(8,128)S(1)}, bf16[8,16,64,4,64]{2,4,1,3,0:T(8,128)(2,1)}) fusion(f32[8,4,64,16,64]{4,2,3,1,0:T(8,128)S(1)} %get-tuple-element.361, f32[8,16,64,4]{2,1,3,0:T(8,128)S(1)} %get-tuple-element.362, pred[16,4]{0,1:T(4,128)(4,1)S(1)} %and_bitcast_fusion.8), kind=kLoop, calls=%fused_computation.15.clone.1 | loop fusion | flops 14639104 | bytes 12877888 | tf_op jit(solution)/shard_map/while/body/eval_jaxpr/reduce_sum | solution.py:24
  254.9 11.4 %copy.122 = bf16[8,16,64,4,64]{4,2,1,3,0:T(8,128)(2,1)} copy(bf16[8,16,64,4,64]{2,4,1,3,0:T(8,128)(2,1)} %get-tuple-element.367) | data formatting | bytes 8388608 | tf_op jit(solution)/shard_map/while/body/eval_jaxpr/convert_element_type | solution.py:27
  266.3 4.9 %fusion.226 = f32[8,4,128,1024]{2,3,1,0:S(1)} fusion(bf16[8,4,64,1024]{2,3,1,0:T(8,128)(2,1)} %bitcast.405, bf16[4,2,64,8,128]{4,2,0,3,1:T(8,128)(2,1)} %bitcast.414), kind=kOutput, calls=%fused_computation.23.clone.1 | convolution fusion | flops 536870912 | bytes 25690112 | tf_op jit(solution)/shard_map/while
  271.2 5.2 %multiply_reduce_fusion.5 = f32[8,16,64,128]{3,2,1,0:T(8,128)S(1)} fusion(f32[8,16,64,4,128]{4,2,1,3,0:T(8,128)S(1)} %bitcast.404, f32[8,16,64,4]{2,1,3,0:T(8,128)S(1)} %get-tuple-element.368), kind=kLoop, calls=%fused_computation.12.clone.1 | loop fusion | flops 7340032 | bytes 21102592 | tf_op jit(solution)/shard_map/while/body/eval_jaxpr/reduce_sum | solution.py:40
  276.4 4.2 multiply_add_fusion.5
  289.5 12.2 %fusion.225 = (f32[8,16,64,4]{2,1,3,0:T(8,128)S(1)}, f32[8,16,64]{2,1,0:T(8,128)S(1)}, bf16[8,16,64,4,64]{2,4,1,3,0:T(8,128)(2,1)}) fusion(f32[8,4,64,16,64]{4,2,3,1,0:T(8,128)S(1)} %get-tuple-element.361, f32[8,16,64,4]{2,1,3,0:T(8,128)S(1)} %get-tuple-element.362, pred[16,4]{0,1:T(4,128)(4,1)S(1)} %and_bitcast_fusion.8), kind=kLoop, calls=%fused_computation.15.clone.1 | loop fusion | flops 14639104 | bytes 12877888 | tf_op jit(solution)/shard_map/while/body/eval_jaxpr/reduce_sum | solution.py:24
  301.9 11.4 %copy.122 = bf16[8,16,64,4,64]{4,2,1,3,0:T(8,128)(2,1)} copy(bf16[8,16,64,4,64]{2,4,1,3,0:T(8,128)(2,1)} %get-tuple-element.367) | data formatting | bytes 8388608 | tf_op jit(solution)/shard_map/while/body/eval_jaxpr/convert_element_type | solution.py:27
  313.3 4.9 %fusion.226 = f32[8,4,128,1024]{2,3,1,0:S(1)} fusion(bf16[8,4,64,1024]{2,3,1,0:T(8,128)(2,1)} %bitcast.405, bf16[4,2,64,8,128]{4,2,0,3,1:T(8,128)(2,1)} %bitcast.414), kind=kOutput, calls=%fused_computation.23.clone.1 | convolution fusion | flops 536870912 | bytes 25690112 | tf_op jit(solution)/shard_map/while
  318.2 5.2 %multiply_reduce_fusion.5 = f32[8,16,64,128]{3,2,1,0:T(8,128)S(1)} fusion(f32[8,16,64,4,128]{4,2,1,3,0:T(8,128)S(1)} %bitcast.404, f32[8,16,64,4]{2,1,3,0:T(8,128)S(1)} %get-tuple-element.368), kind=kLoop, calls=%fused_computation.12.clone.1 | loop fusion | flops 7340032 | bytes 21102592 | tf_op jit(solution)/shard_map/while/body/eval_jaxpr/reduce_sum | solution.py:40
  323.4 4.2 multiply_add_fusion.5
  336.5 12.2 %fusion.225 = (f32[8,16,64,4]{2,1,3,0:T(8,128)S(1)}, f32[8,16,64]{2,1,0:T(8,128)S(1)}, bf16[8,16,64,4,64]{2,4,1,3,0:T(8,128)(2,1)}) fusion(f32[8,4,64,16,64]{4,2,3,1,0:T(8,128)S(1)} %get-tuple-element.361, f32[8,16,64,4]{2,1,3,0:T(8,128)S(1)} %get-tuple-element.362, pred[16,4]{0,1:T(4,128)(4,1)S(1)} %and_bitcast_fusion.8), kind=kLoop, calls=%fused_computation.15.clone.1 | loop fusion | flops 14639104 | bytes 12877888 | tf_op jit(solution)/shard_map/while/body/eval_jaxpr/reduce_sum | solution.py:24
  348.9 11.4 %copy.122 = bf16[8,16,64,4,64]{4,2,1,3,0:T(8,128)(2,1)} copy(bf16[8,16,64,4,64]{2,4,1,3,0:T(8,128)(2,1)} %get-tuple-element.367) | data formatting | bytes 8388608 | tf_op jit(solution)/shard_map/while/body/eval_jaxpr/convert_element_type | solution.py:27
  360.3 4.9 %fusion.226 = f32[8,4,128,1024]{2,3,1,0:S(1)} fusion(bf16[8,4,64,1024]{2,3,1,0:T(8,128)(2,1)} %bitcast.405, bf16[4,2,64,8,128]{4,2,0,3,1:T(8,128)(2,1)} %bitcast.414), kind=kOutput, calls=%fused_computation.23.clone.1 | convolution fusion | flops 536870912 | bytes 25690112 | tf_op jit(solution)/shard_map/while
  365.2 5.2 %multiply_reduce_fusion.5 = f32[8,16,64,128]{3,2,1,0:T(8,128)S(1)} fusion(f32[8,16,64,4,128]{4,2,1,3,0:T(8,128)S(1)} %bitcast.404, f32[8,16,64,4]{2,1,3,0:T(8,128)S(1)} %get-tuple-element.368), kind=kLoop, calls=%fused_computation.12.clone.1 | loop fusion | flops 7340032 | bytes 21102592 | tf_op jit(solution)/shard_map/while/body/eval_jaxpr/reduce_sum | solution.py:40
  383.5 12.2 %fusion.225 = (f32[8,16,64,4]{2,1,3,0:T(8,128)S(1)}, f32[8,16,64]{2,1,0:T(8,128)S(1)}, bf16[8,16,64,4,64]{2,4,1,3,0:T(8,128)(2,1)}) fusion(f32[8,4,64,16,64]{4,2,3,1,0:T(8,128)S(1)} %get-tuple-element.361, f32[8,16,64,4]{2,1,3,0:T(8,128)S(1)} %get-tuple-element.362, pred[16,4]{0,1:T(4,128)(4,1)S(1)} %and_bitcast_fusion.8), kind=kLoop, calls=%fused_computation.15.clone.1 | loop fusion | flops 14639104 | bytes 12877888 | tf_op jit(solution)/shard_map/while/body/eval_jaxpr/reduce_sum | solution.py:24
  395.9 11.4 %copy.122 = bf16[8,16,64,4,64]{4,2,1,3,0:T(8,128)(2,1)} copy(bf16[8,16,64,4,64]{2,4,1,3,0:T(8,128)(2,1)} %get-tuple-element.367) | data formatting | bytes 8388608 | tf_op jit(solution)/shard_map/while/body/eval_jaxpr/convert_element_type | solution.py:27
  407.3 4.9 %fusion.226 = f32[8,4,128,1024]{2,3,1,0:S(1)} fusion(bf16[8,4,64,1024]{2,3,1,0:T(8,128)(2,1)} %bitcast.405, bf16[4,2,64,8,128]{4,2,0,3,1:T(8,128)(2,1)} %bitcast.414), kind=kOutput, calls=%fused_computation.23.clone.1 | convolution fusion | flops 536870912 | bytes 25690112 | tf_op jit(solution)/shard_map/while
  412.1 5.2 %multiply_reduce_fusion.5 = f32[8,16,64,128]{3,2,1,0:T(8,128)S(1)} fusion(f32[8,16,64,4,128]{4,2,1,3,0:T(8,128)S(1)} %bitcast.404, f32[8,16,64,4]{2,1,3,0:T(8,128)S(1)} %get-tuple-element.368), kind=kLoop, calls=%fused_computation.12.clone.1 | loop fusion | flops 7340032 | bytes 21102592 | tf_op jit(solution)/shard_map/while/body/eval_jaxpr/reduce_sum | solution.py:40
  426.6 26.0 %all_to_all.63 = bf16[1024,8,128]{2,1,0:T(8,128)(2,1)S(1)} all-to-all(bf16[1024,8,128]{2,1,0:T(8,128)(2,1)S(1)} %bitcast.437), channel_id=1, replica_groups=mesh['head'=2,'frame'=16] {'head'}, dimensions={0} | all-to-all | bytes 4194304 | tf_op jit(solution)/shard_map/all_to_all | solution.py:162
  (247 shorter events, 155.5 us)
Async XLA Ops:
  6.5 20.2 %copy-start = (s32[16,16,16]{2,1,0:T(8,128)S(1)}, s32[16,16,16]{2,1,0:T(8,128)}, u32[]{:S(2)}) copy-start(s32[16,16,16]{2,1,0:T(8,128)} %param.13) | copy-start | bytes 49156
  6.5 7.3 %copy-start.2 = (s32[16]{0:T(128)S(1)}, s32[16]{0:T(128)}, u32[]{:S(2)}) copy-start(s32[16]{0:T(128)} %param.15) | copy-start | bytes 196
  6.5 19.5 %copy-start.3 = (s32[16]{0:T(128)S(1)}, s32[16]{0:T(128)}, u32[]{:S(2)}) copy-start(s32[16]{0:T(128)} %param.14) | copy-start | bytes 196
  10.0 31.8 %all-to-all-start.1 = ((bf16[512,16,128]{2,0,1:T(8,128)(2,1)}), bf16[512,16,128]{2,0,1:T(8,128)(2,1)S(1)}, u32[]{:S(2)}, u32[]{:S(2)}) async-start(bf16[512,16,128]{2,0,1:T(8,128)(2,1)} %copy.74), calls=%async_computation.1 | async-start | bytes 4194304 | tf_op jit(solution)/shard_map/all_to_all | solution.py:53
  41.9 29.2 %all-to-all-start.2 = ((bf16[512,16,128]{2,0,1:T(8,128)(2,1)}), bf16[512,16,128]{2,0,1:T(8,128)(2,1)}, u32[]{:S(2)}, u32[]{:S(2)}) async-start(bf16[512,16,128]{2,0,1:T(8,128)(2,1)} %copy.79), calls=%async_computation.2 | async-start | bytes 4194304 | tf_op jit(solution)/shard_map/all_to_all | solution.py:54
  71.0 28.2 %all-to-all-start = ((bf16[512,16,128]{2,0,1:T(8,128)(2,1)}), bf16[512,16,128]{2,0,1:T(8,128)(2,1)}, u32[]{:S(2)}, u32[]{:S(2)}) async-start(bf16[512,16,128]{2,0,1:T(8,128)(2,1)} %copy.73), calls=%async_computation | async-start | bytes 4194304 | tf_op jit(solution)/shard_map/all_to_all | solution.py:52
  75.9 157.5 %all-gather.3.cloned.1.call-start = ((), (), s32[]{:S(2)}) async-start(), calls=%async_computation.4 | async-start | bytes 4456448 | tf_op jit(solution)/shard_map/all_gather | solution.py:134
  90.4 52.5 %collective-permute-start.3 = (bf16[2,4,64,8,128]{4,3,2,1,0:T(8,128)(2,1)}, bf16[2,4,64,8,128]{4,3,2,1,0:T(8,128)(2,1)}, u32[]{:S(2)}, u32[]{:S(2)}) collective-permute-start(bf16[2,4,64,8,128]{4,3,2,1,0:T(8,128)(2,1)} %pad_maximum_fusion), channel_id=1, source_target_pairs={{1,0},{2,1},{3,2},{4,3},{5,4},{6,5},{7,6},{8,7},{9,8},{10,9},{11,1... | collective-permute-start | bytes 3145736 | tf_op jit(solution)/shard_map/ppermute | solution.py:12
  93.8 56.1 %collective-permute-start = (bf16[2,4,64,8,128]{4,3,2,1,0:T(8,128)(2,1)}, bf16[2,4,64,8,128]{4,3,2,1,0:T(8,128)(2,1)}, u32[]{:S(2)}, u32[]{:S(2)}) collective-permute-start(bf16[2,4,64,8,128]{4,3,2,1,0:T(8,128)(2,1)} %pad_maximum_fusion), channel_id=1, source_target_pairs={{0,1},{1,2},{2,3},{3,4},{4,5},{5,6},{6,7},{7,8},{8,9},{9,10},{10,1... | collective-permute-start | bytes 3145736 | tf_op jit(solution)/shard_map/ppermute | solution.py:12
  144.1 30.3 %collective-permute-start.4 = (bf16[2,2,64,8,128]{4,2,1,3,0:T(8,128)(2,1)S(1)}, bf16[2,2,64,8,128]{4,2,1,3,0:T(8,128)(2,1)S(1)}, u32[]{:S(2)}, u32[]{:S(2)}) collective-permute-start(bf16[2,2,64,8,128]{4,2,1,3,0:T(8,128)(2,1)S(1)} %bitcast.462), channel_id=1, source_target_pairs={{1,0},{2,1},{3,2},{4,3},{5,4},{6,5},{7,6},{8,7},{9,8},{10,9},{11,1... | collective-permute-start | bytes 1572872 | tf_op jit(solution)/shard_map/ppermute | solution.py:12
  151.2 22.4 %collective-permute-start.1 = (bf16[2,2,64,8,128]{4,2,1,3,0:T(8,128)(2,1)S(1)}, bf16[2,2,64,8,128]{4,2,1,3,0:T(8,128)(2,1)S(1)}, u32[]{:S(2)}, u32[]{:S(2)}) collective-permute-start(bf16[2,2,64,8,128]{4,2,1,3,0:T(8,128)(2,1)S(1)} %bitcast.464), channel_id=1, source_target_pairs={{0,1},{1,2},{2,3},{3,4},{4,5},{5,6},{6,7},{7,8},{8,9},{9,10},{10,1... | collective-permute-start | bytes 1572872 | tf_op jit(solution)/shard_map/ppermute | solution.py:12
  176.3 18.1 %collective-permute-start.5 = (bf16[2,2,64,8,128]{4,2,1,3,0:T(8,128)(2,1)S(1)}, bf16[2,2,64,8,128]{4,2,1,3,0:T(8,128)(2,1)S(1)}, u32[]{:S(2)}, u32[]{:S(2)}) collective-permute-start(bf16[2,2,64,8,128]{4,2,1,3,0:T(8,128)(2,1)S(1)} %collective-permute-done.4), channel_id=1, source_target_pairs={{1,0},{2,1},{3,2},{4,3},{5,4},{6,5},{7,6},{8,7},{9,8},{10,9},{11,1... | collective-permute-start | bytes 1572872 | tf_op jit(solution)/shard_map/ppermute | solution.py:12
  187.4 13.7 %collective-permute-start.2 = (bf16[2,2,64,8,128]{4,2,1,3,0:T(8,128)(2,1)S(1)}, bf16[2,2,64,8,128]{4,2,1,3,0:T(8,128)(2,1)S(1)}, u32[]{:S(2)}, u32[]{:S(2)}) collective-permute-start(bf16[2,2,64,8,128]{4,2,1,3,0:T(8,128)(2,1)S(1)} %collective-permute-done.1), channel_id=1, source_target_pairs={{0,1},{1,2},{2,3},{3,4},{4,5},{5,6},{6,7},{7,8},{8,9},{9,10},{10,1... | collective-permute-start | bytes 1572872 | tf_op jit(solution)/shard_map/ppermute | solution.py:12
  210.1 2.7 copy-start.7
  210.2 2.7 copy-start.8
  238.6 3.9 copy-start.4
  254.9 11.4 %copy-start.5 = (f32[8,16,64]{2,1,0:T(8,128)}, f32[8,16,64]{2,1,0:T(8,128)S(1)}, u32[]{:S(2)}) copy-start(f32[8,16,64]{2,1,0:T(8,128)S(1)} %get-tuple-element.398) | copy-start | bytes 98308 | tf_op jit(solution)/shard_map/while
  276.4 4.2 copy-start.6
  285.6 3.9 copy-start.4
  301.9 11.4 %copy-start.5 = (f32[8,16,64]{2,1,0:T(8,128)}, f32[8,16,64]{2,1,0:T(8,128)S(1)}, u32[]{:S(2)}) copy-start(f32[8,16,64]{2,1,0:T(8,128)S(1)} %get-tuple-element.398) | copy-start | bytes 98308 | tf_op jit(solution)/shard_map/while
  323.4 4.2 copy-start.6
  332.6 3.9 copy-start.4
  348.9 11.4 %copy-start.5 = (f32[8,16,64]{2,1,0:T(8,128)}, f32[8,16,64]{2,1,0:T(8,128)S(1)}, u32[]{:S(2)}) copy-start(f32[8,16,64]{2,1,0:T(8,128)S(1)} %get-tuple-element.398) | copy-start | bytes 98308 | tf_op jit(solution)/shard_map/while
  370.4 4.2 copy-start.6
  379.6 3.9 copy-start.4
  395.9 11.4 %copy-start.5 = (f32[8,16,64]{2,1,0:T(8,128)}, f32[8,16,64]{2,1,0:T(8,128)S(1)}, u32[]{:S(2)}) copy-start(f32[8,16,64]{2,1,0:T(8,128)S(1)} %get-tuple-element.398) | copy-start | bytes 98308 | tf_op jit(solution)/shard_map/while
  417.3 4.2 copy-start.6
  426.5 27.7 %copy-start.1 = (s32[16,16,16]{2,1,0:T(8,128)S(1)}, s32[16,16,16]{2,1,0:T(8,128)}, u32[]{:S(2)}) copy-start(s32[16,16,16]{2,1,0:T(8,128)} %param.13) | copy-start | bytes 49156
Sparse Core Ops, SparseCore 0:
  143.0 56.4 all-gather.2
where the time goes:
time: 470 us; the launch traced here: 462 us
  other arithmetic  134 us (29%)
  local copies, waits for them, and re-layouts  106 us (23%)
  matrix products  99.9 us (21%)
  starting transfers between devices  34.8 us (7%)
  between operations  31.8 us (7%)
  waiting for transfers between devices  26.5 us (6%)
  blocking collectives  26 us (6%)
    reduce_sum x11, other arithmetic, group_terms(): group_totals = jnp.sum(weights, axis=4)  76.7 us
    dot_general x8, matrix products, group_terms(): jnp.einsum('hqagn,gnhd->hqagd', weights.astype(jnp.bfloat16), value_rows,...  49.6 us
    convert_element_type x4, local copies, waits for them, and re-layouts, group_terms(): weights.astype(jnp.bfloat16)  45.5 us
    all_to_all x1, blocking collectives, local(): lax.all_to_all(output, 'head', split_axis=0, concat_axis=1, tiled=True)  26 us
    dot_general x6, matrix products, group_terms(): jnp.einsum('qahd,gnhd->hqagn', query_blocks, key_rows, preferred_element_...  25.4 us
    ppermute x6, starting transfers between devices, passed_along(): return lax.ppermute(block, axis, route)  21.3 us
    reduce_sum x4, other arithmetic, absorb(): jnp.sum(factors[..., None] * group_sums, axis=3)  20.8 us
    while x4, matrix products  19.5 us
  transfers between devices with their start and end apart: 10, of which 3 were waited for; matrix products, arithmetic and copies ran while one was open for 31% of the time, Pallas kernels for 0%

commit v1 on v0

v1 whole, which is shorter than its diff:
```python
import functools
import math

import jax
import jax.numpy as jnp
from jax import lax
from jax.experimental import pallas as pl
from jax.experimental.pallas import tpu as pltpu
from jax.sharding import PartitionSpec as P

masked_score = -1e30
lanes = 128
vmem_bytes = 48 * 1024 * 1024


def rotated(block, axis, shift):
    size = lax.axis_size(axis)
    return lax.ppermute(block, axis, [(i, (i + shift) % size) for i in range(size)])


def passed_along(block, axis, distance):
    devices = range(lax.axis_size(axis))
    route = [(i - distance, i) for i in devices if i - distance in devices]
    return lax.ppermute(block, axis, route)


def query_rows(q_ref, start, first_row, tile, block_rows):
    query = q_ref[start : start + tile, :]
    row = lax.broadcasted_iota(jnp.int32, (tile, lanes), 0) + first_row
    lane = lax.broadcasted_iota(jnp.int32, (tile, lanes), 1)
    marks = jnp.where(row // block_rows == lane, 1.0, 0.0).astype(jnp.bfloat16)
    return jnp.concatenate([query, marks], axis=1)


def score_tile(query_marked, keys_marked):
    return lax.dot_general(
        query_marked, keys_marked, (((1,), (1,)), ((), ())), preferred_element_type=jnp.float32
    )


def own_kernel(parts, tile, block_rows, factor, start_ref, bias_ref, *refs):
    q_refs, k_refs, v_refs = refs[:parts], refs[parts : 2 * parts], refs[2 * parts : 3 * parts]
    state_ref = refs[3 * parts]
    key_rows = jnp.concatenate([ref[...] for ref in k_refs], axis=0)
    value_rows = jnp.concatenate([ref[...] for ref in v_refs], axis=0)
    keys_marked = jnp.concatenate([key_rows, bias_ref[...]], axis=1)
    values_ones = jnp.concatenate([value_rows, jnp.ones_like(value_rows)], axis=1)
    rows, head_dim = q_refs[0].shape
    for part in range(parts):
        for start in range(0, rows, tile):
            first_row = part * rows + start
            marked = query_rows(q_refs[part], start, first_row, tile, block_rows)
            scores = score_tile(marked, keys_marked)
            top = jnp.max(scores, axis=1, keepdims=True)
            weights = jnp.exp2(scores * factor - top * factor).astype(jnp.bfloat16)
            sums = jnp.dot(weights, values_ones, preferred_element_type=jnp.float32)
            lane = lax.broadcasted_iota(jnp.int32, (tile, head_dim), 1)
            state_ref[first_row : first_row + tile, :head_dim] = sums[:, :head_dim]
            state_ref[first_row : first_row + tile, head_dim:] = jnp.where(
                lane < head_dim // 2, sums[:, head_dim:], top
            )


def near_kernel(parts, sources, tile, block_rows, factor, start_ref, bias_ref, *refs):
    q_refs = refs[:parts]
    state_ref = refs[parts]
    k_refs = refs[parts + 1 : parts + 1 + sources]
    v_refs = refs[parts + 1 + sources : parts + 1 + 2 * sources]
    out_refs = refs[parts + 1 + 2 * sources :]
    rows, head_dim = q_refs[0].shape
    key_rows = jnp.concatenate([ref[...].reshape(-1, head_dim) for ref in k_refs], axis=0)
    value_rows = jnp.concatenate([ref[...].reshape(-1, head_dim) for ref in v_refs], axis=0)
    keys_marked = jnp.concatenate([key_rows, bias_ref[...]], axis=1)
    values_ones = jnp.concatenate([value_rows, jnp.ones_like(value_rows)], axis=1)
    for part in range(parts):
        for start in range(0, rows, tile):
            first_row = part * rows + start
            marked = query_rows(q_refs[part], start, first_row, tile, block_rows)
            scores = score_tile(marked, keys_marked)
            state = state_ref[first_row : first_row + tile, :]
            own_total = state[:, head_dim : head_dim + 1]
            own_top = state[:, 2 * head_dim - 1 :]
            top = jnp.maximum(jnp.max(scores, axis=1, keepdims=True), own_top)
            weights = jnp.exp2(scores * factor - top * factor).astype(jnp.bfloat16)
            sums = jnp.dot(weights, values_ones, preferred_element_type=jnp.float32)
            shrink = jnp.exp2(own_top * factor - top * factor)
            total = own_total * shrink + sums[:, head_dim : head_dim + 1]
            result = (state[:, :head_dim] * shrink + sums[:, :head_dim]) / total
            out_refs[part][start : start + tile, :] = result.astype(jnp.bfloat16)


def local(queries, keys, values, block_mask, strides, offsets):
    parts = lax.axis_size("head")
    frame_total = lax.axis_size("frame")
    here = lax.axis_index("head")
    frame_index = lax.axis_index("frame")
    rows, heads, head_dim = queries.shape
    frame_blocks = block_mask.shape[1]
    heads_here = heads // parts
    part_blocks = frame_blocks // parts
    block_rows = rows // part_blocks
    wide, narrow = frame_blocks // 4, frame_blocks // 2
    group_heads = min(2, heads_here)
    groups = heads_here // group_heads
    tile = min(256, rows)
    factor = head_dim ** (-0.5) * math.log2(math.e)
    early = part_blocks % narrow == 0

    packed = jnp.transpose(jnp.stack([keys, values, queries]), (0, 2, 1, 3))

    def head_slab(array, device, first, count):
        return lax.dynamic_slice_in_dim(array, device * heads_here + first, count, axis=1)

    part_ids = (here - jnp.arange(parts, dtype=jnp.int32)) % parts
    own_ids = (part_ids[:, None] * part_blocks + jnp.arange(part_blocks, dtype=jnp.int32)).reshape(-1)

    def slots(spacing):
        if early:
            inside = spacing * jnp.arange(part_blocks // spacing, dtype=jnp.int32)
            return (part_ids[:, None] * part_blocks + inside).reshape(-1)
        return spacing * jnp.arange(frame_blocks // spacing, dtype=jnp.int32)

    def firsts(spacing, frames):
        return (spacing - offsets[frames] % spacing) % spacing

    def exchange(slab_of):
        return [rotated(slab_of((here + s) % parts), "head", s) for s in range(1, parts)]

    my_wide = firsts(wide, frame_index)
    my_narrow = firsts(narrow, frame_index)
    my_anchor = firsts(frame_blocks, frame_index)
    if early:
        cut = packed[:2].reshape(2, heads, part_blocks // wide, wide, block_rows, head_dim)
        cut = lax.dynamic_index_in_dim(cut, my_wide, 3, keepdims=False)
        candidates = [head_slab(cut, here, 0, heads_here)]
        candidates += exchange(lambda device: head_slab(cut, device, 0, heads_here))
        candidates = jnp.stack(candidates, axis=2)

    arrived = []
    for group in range(groups):
        arrived.append(
            exchange(lambda device: head_slab(packed, device, group * group_heads, group_heads))
        )

    if early:
        wide_pack = candidates.reshape(2, heads_here, -1, head_dim)
        split = candidates.reshape(
            2, heads_here, parts * part_blocks // narrow, 2, block_rows, head_dim
        )
        narrow_pack = lax.dynamic_index_in_dim(split, my_narrow // wide, 3, keepdims=False)
        narrow_pack = narrow_pack.reshape(2, heads_here, -1, head_dim)
        anchor_part = (here - my_anchor // part_blocks) % parts
        anchor_spot = anchor_part * (part_blocks // wide) + (my_anchor % part_blocks) // wide
        anchor_pack = lax.dynamic_slice_in_dim(wide_pack, anchor_spot * block_rows, block_rows, axis=2)
    else:
        mine = head_slab(packed[:2], here, 0, heads_here)
        theirs = [
            jnp.concatenate([arrived[g][s][:2] for g in range(groups)], axis=1)
            for s in range(parts - 1)
        ]
        whole = jnp.stack([mine] + theirs, axis=2)
        whole = whole.reshape(2, heads_here, frame_blocks, block_rows, head_dim)

        def picked(ids):
            spots = (here - ids // part_blocks) % parts * part_blocks + ids % part_blocks
            return jnp.take(whole, spots, axis=2).reshape(2, heads_here, -1, head_dim)

        wide_pack = picked(my_wide + slots(wide))
        narrow_pack = picked(my_narrow + slots(narrow))
        anchor_pack = picked(my_anchor[None])

    gathered = lax.all_gather(anchor_pack, "frame", axis=0, tiled=False)
    sources = []
    id_lists, flag_lists = [own_ids], [jnp.ones((frame_blocks,), jnp.bool_)]
    for distance in (1, 2, 3):
        spacing = wide if distance == 1 else narrow
        for direction in (1, -1):
            pack = wide_pack if distance == 1 else narrow_pack
            sources.append(passed_along(pack, "frame", direction * distance))
            source = frame_index - direction * distance
            valid = (source >= 0) & (source < frame_total)
            clipped = jnp.clip(source, 0, frame_total - 1)
            chosen = firsts(spacing, clipped) + slots(spacing)
            id_lists.append(chosen)
            flag_lists.append(valid & ((chosen + offsets[clipped]) % strides[distance] == 0))
    frames = jnp.arange(frame_total, dtype=jnp.int32)
    spots = firsts(frame_blocks, frames)
    gaps = jnp.abs(frame_index - frames)
    id_lists.append(spots)
    flag_lists.append((gaps >= 4) & ((spots + offsets) % frame_blocks == 0))
    ids = jnp.concatenate(id_lists)
    flags = jnp.concatenate(flag_lists)

    own_mask = lax.dynamic_index_in_dim(block_mask, frame_index, 0, keepdims=False)
    kept = jnp.take(jnp.take(own_mask, own_ids, axis=0), ids, axis=1) == 1
    bias = jnp.where(kept & flags[None, :], 0.0, masked_score).astype(jnp.bfloat16).T
    bias = jnp.pad(bias, ((0, 0), (0, lanes - frame_blocks)))
    bias = jnp.repeat(bias, block_rows, axis=0)
    own_bias, near_bias = bias[: frame_blocks * block_rows], bias[frame_blocks * block_rows :]

    def scalar_grid(in_specs, out_specs):
        return pltpu.PrefetchScalarGridSpec(
            num_scalar_prefetch=1, grid=(group_heads,), in_specs=in_specs, out_specs=out_specs
        )

    def whole_block(array):
        return pl.BlockSpec(array.shape, lambda h, start: (0, 0))

    def own_block(which):
        return pl.BlockSpec(
            (None, None, rows, head_dim), lambda h, start: (which, start[0] + h, 0, 0)
        )

    def part_block(which):
        return pl.BlockSpec((None, None, rows, head_dim), lambda h, start: (which, h, 0, 0))

    params = pltpu.CompilerParams(vmem_limit_bytes=vmem_bytes)
    all_rows = parts * rows
    state_block = pl.BlockSpec((None, all_rows, 2 * head_dim), lambda h, start: (h, 0, 0))
    states, starts = [], []
    for group in range(groups):
        starts.append((here * heads_here + group * group_heads).reshape(1).astype(jnp.int32))
        blocks, operands = [], []
        for which in (2, 0, 1):
            blocks += [own_block(which)] + [part_block(which)] * (parts - 1)
            operands += [packed] + arrived[group]
        states.append(
            pl.pallas_call(
                functools.partial(own_kernel, parts, tile, block_rows, factor),
                grid_spec=scalar_grid([whole_block(own_bias)] + blocks, state_block),
                out_shape=jax.ShapeDtypeStruct(
                    (group_heads, all_rows, 2 * head_dim), jnp.float32
                ),
                compiler_params=params,
                cost_estimate=pl.CostEstimate(
                    flops=group_heads * 8 * all_rows * all_rows * head_dim,
                    bytes_accessed=group_heads * all_rows * head_dim * 14,
                    transcendentals=group_heads * all_rows * all_rows,
                ),
            )(starts[group], own_bias, *operands)
        )

    finished = []
    near_rows = near_bias.shape[0]
    for group in range(groups):
        base = group * group_heads

        def near_block(which, array):
            return pl.BlockSpec(
                (None, None) + array.shape[2:], lambda h, start: (which, base + h, 0, 0)
            )

        def anchor_block(which):
            return pl.BlockSpec(
                (frame_total, None, None, block_rows, head_dim),
                lambda h, start: (0, which, base + h, 0, 0),
            )

        blocks = [whole_block(near_bias), own_block(2)] + [part_block(2)] * (parts - 1)
        operands = [near_bias, packed] + arrived[group]
        blocks.append(state_block)
        operands.append(states[group])
        for which in (0, 1):
            blocks += [near_block(which, array) for array in sources] + [anchor_block(which)]
            operands += sources + [gathered]
        out_block = pl.BlockSpec((None, rows, head_dim), lambda h, start: (h, 0, 0))
        outs = pl.pallas_call(
            functools.partial(near_kernel, parts, len(sources) + 1, tile, block_rows, factor),
            grid_spec=scalar_grid(blocks, [out_block] * parts),
            out_shape=[jax.ShapeDtypeStruct((group_heads, rows, head_dim), jnp.bfloat16)] * parts,
            compiler_params=params,
            cost_estimate=pl.CostEstimate(
                flops=group_heads * 8 * all_rows * near_rows * head_dim,
                bytes_accessed=group_heads * (all_rows * 14 + near_rows * 4) * head_dim,
                transcendentals=group_heads * all_rows * near_rows,
            ),
        )(starts[group], *operands)
        finished.append([outs[0]] + [rotated(outs[p], "head", -p) for p in range(1, parts)])

    stacked = jnp.stack(
        [jnp.concatenate([entry[p] for entry in finished], axis=0) for p in range(parts)]
    )
    order = (jnp.arange(parts, dtype=jnp.int32) - here) % parts
    output = jnp.take(stacked, order, axis=0).reshape(heads, rows, head_dim)
    return jnp.transpose(output, (1, 0, 2))


def solution(mesh):
    placed = (
        P(("frame", "head"), None, None),
        P(("frame", "head"), None, None),
        P(("frame", "head"), None, None),
        P(),
        P(),
        P(),
    )
    return jax.shard_map(
        local,
        mesh=mesh,
        in_specs=placed,
        out_specs=P(("frame", "head"), None, None),
        check_vma=False,
    )
```

time: 470 us -> 226 us (0.48)
  the two profiles are of different devices: /device:TPU:3 before, /device:TPU:26 now
where the time goes in v1:
time: 226 us; the launch traced here: 225 us
  Pallas kernels  55.7 us (25%)
  starting transfers between devices  44.5 us (20%)
  local copies, waits for them, and re-layouts  39 us (17%)
  waiting for transfers between devices  38 us (17%)
  between operations  31.3 us (14%)
  other arithmetic  16.9 us (7%)
    ppermute x9, waiting for transfers between devices, rotated(): lax.ppermute(block, axis, [(i, (i + shift) % size) for i in range(size)])  38 us
    pallas_call x4, Pallas kernels, local(): pl.pallas_call(functools.partial(near_kernel, parts, len(sources) + 1, ti...  36.2 us
    ppermute x6, starting transfers between devices, passed_along(): return lax.ppermute(block, axis, route)  34.8 us
    unnamed x53, local copies, waits for them, and re-layouts  22.4 us
    pallas_call x4, Pallas kernels, local(): pl.pallas_call(functools.partial(own_kernel, parts, tile, block_rows, fac...  19.5 us
    ppermute x9, starting transfers between devices, rotated(): lax.ppermute(block, axis, [(i, (i + shift) % size) for i in range(size)])  9.69 us
    dynamic_slice x4, local copies, waits for them, and re-layouts, head_slab(): lax.dynamic_slice_in_dim(array, device * heads_here + first, count, axis=1)  4.94 us
  transfers between devices with their start and end apart: 16, of which 5 were waited for; matrix products, arithmetic and copies ran while one was open for 7% of the time, Pallas kernels for 21%

profile of v1, /device:TPU:26, one launch (start us, length us, event | category | flops | bytes accessed | tf_op | source)
XLA Modules:
  0.0 225.5 jit_solution(770233020383999892)
XLA Ops:
  6.5 1.6 fusion.15
  10.1 2.3 %copy.39 = bf16[512,16,128]{2,0,1:T(8,128)(2,1)S(1)} copy(bf16[512,16,128]{2,1,0:T(8,128)(2,1)} %param.7) | data formatting | bytes 4194304 | tf_op args[1]
  14.1 3.4 %pad_maximum_fusion = (bf16[3,512,16,128]{3,1,2,0:T(8,128)(2,1)}, bf16[3,16,512,128]{3,2,1,0:T(8,128)(2,1)S(1)}) fusion(bf16[1,512,16,128]{3,1,2,0:T(8,128)(2,1)S(1)} %get-tuple-element.58, bf16[1,512,16,128]{3,1,2,0:T(8,128)(2,1)S(1)} %get-tuple-element.59, bf16[1,512,16,128]{3,1,2,0:T(8,128)(2,1)S(1)} %bitcast.80), kind=kLoop, calls=%fused_computation.4 | loop fusion | flops 6291456 | bytes 18874368 | tf_op jit(solution)/shard_map/stack | solution.py:109
  17.5 2.7 %copy-done.19 = bf16[3,16,512,128]{3,2,1,0:T(8,128)(2,1)} copy-done((bf16[3,16,512,128]{3,2,1,0:T(8,128)(2,1)}, bf16[3,16,512,128]{3,2,1,0:T(8,128)(2,1)S(1)}, u32[]{:S(2)}) %copy-start.19) | copy-done | bytes 6291480
  20.2 2.4 %slice.45 = bf16[2,16,512,128]{3,2,1,0:T(8,128)(2,1)} slice(bf16[3,16,512,128]{3,2,1,0:T(8,128)(2,1)S(1)} %get-tuple-element.36.refs_0_.refs_2_.refs_4_), slice={[0:2], [0:16], [0:512], [0:128]} | slice | bytes 8388608 | tf_op jit(solution)/shard_map/slice | solution.py:133
  23.9 1.6 collective-permute-start.1
  25.5 12.1 %collective-permute-done.1 = bf16[2,8,2,64,128]{4,3,1,0,2:T(8,128)(2,1)S(1)} collective-permute-done((bf16[2,8,2,64,128]{4,3,1,0,2:T(8,128)(2,1)S(1)}, bf16[2,8,2,64,128]{4,3,1,0,2:T(8,128)(2,1)S(1)}, u32[]{:S(2)}, u32[]{:S(2)}) %collective-permute-start.1) | collective-permute-done | bytes 524320 | tf_op jit(solution)/shard_map/ppermute | solution.py:18
  40.3 3.6 %dynamic-slice_bitcast_fusion.3 = (bf16[3,2,512,128]{3,2,1,0:T(8,128)(2,1)}, bf16[3,2,512,128]{3,2,1,0:T(8,128)(2,1)}, bf16[3,2,512,128]{3,2,1,0:T(8,128)(2,1)}, bf16[3,2,512,128]{3,2,1,0:T(8,128)(2,1)}) fusion(bf16[3,512,16,128]{3,1,2,0:T(8,128)(2,1)} %get-tuple-element.35, s32[]{:T(128)S(6)} %select_n.412, s32[]{:T(128)S(6)} %select_n.432, ...), kind=kLoop, calls=%fused_computation.19 | loop fusion | bytes 6291472 | tf_op jit(solution)/shard_map/dynamic_slice | solution.py:112
  43.9 1.5 collective-permute-start.10
  45.9 1.5 collective-permute-start.8
  69.7 1.5 compare_and_fusion.5
  71.4 1.9 collective-permute-start.2
  73.3 1.8 fusion.1
  76.1 3.6 %collective-permute-start.3 = (bf16[2,8,256,128]{3,2,1,0:T(8,128)(2,1)}, bf16[2,8,256,128]{3,2,1,0:T(8,128)(2,1)S(1)}, u32[]{:S(2)}, u32[]{:S(2)}) collective-permute-start(bf16[2,8,256,128]{3,2,1,0:T(8,128)(2,1)} %bitcast.89), channel_id=1, source_target_pairs={{1,0},{2,1},{3,2},{4,3},{5,4},{6,5},{7,6},{8,7},{9,8},{10,9},{11,1... | collective-permute-start | bytes 3145736 | tf_op jit(solution)/shard_map/ppermute | solution.py:24
  79.7 1.8 collective-permute-done.9.refs_1_.refs_3_.refs_5_
  84.1 4.8 %shard_map.70.refs_2_ = f32[2,1024,256]{2,1,0:T(8,128)S(1)} custom-call(s32[1]{0:T(128)} %bitcast.37.start_ref, bf16[1024,128]{1,0:T(8,128)(2,1)S(1)} %bitcast.68, bf16[3,16,512,128]{3,2,1,0:T(8,128)(2,1)} %copy-done.19, bf16[3,2,512,128]{3,2,1,0:T(8,128)(2,1)S(1)} %copy-done.10, bf16[3,16,512,128]{3,2,1,0:T(8,128)(2,1)} %copy-done.19, ...), custom_call_target="tpu_custom_call" | custom-call | flops 2147483648 | bytes 3670016 | tf_op jit(solution)/shard_map/pallas_call | solution.py:228
  90.2 8.0 %collective-permute-done.8.refs_1_.refs_3_.refs_5_ = bf16[3,2,512,128]{3,2,1,0:T(8,128)(2,1)S(1)} collective-permute-done((bf16[3,2,512,128]{3,2,1,0:T(8,128)(2,1)}, bf16[3,2,512,128]{3,2,1,0:T(8,128)(2,1)S(1)}, u32[]{:S(2)}, u32[]{:S(2)}) %collective-permute-start.8) | collective-permute-done | bytes 786464 | tf_op jit(solution)/shard_map/ppermute | solution.py:18
  99.1 2.5 %collective-permute-start.5 = (bf16[2,8,128,128]{3,2,1,0:T(8,128)(2,1)}, bf16[2,8,128,128]{3,2,1,0:T(8,128)(2,1)S(1)}, u32[]{:S(2)}, u32[]{:S(2)}) collective-permute-start(bf16[2,8,128,128]{3,2,1,0:T(8,128)(2,1)} %bitcast.31), channel_id=1, source_target_pairs={{2,0},{3,1},{4,2},{5,3},{6,4},{7,5},{8,6},{9,7},{10,8},{11,9},{12,... | collective-permute-start | bytes 1572872 | tf_op jit(solution)/shard_map/ppermute | solution.py:24
  101.6 11.5 %collective-permute-done.refs_1_.refs_3_.refs_5_ = bf16[3,2,512,128]{3,2,1,0:T(8,128)(2,1)} collective-permute-done((bf16[3,2,512,128]{3,2,1,0:T(8,128)(2,1)}, bf16[3,2,512,128]{3,2,1,0:T(8,128)(2,1)}, u32[]{:S(2)}, u32[]{:S(2)}) %collective-permute-start) | collective-permute-done | bytes 786464 | tf_op jit(solution)/shard_map/ppermute | solution.py:18
  114.4 24.2 %collective-permute-start.7 = (bf16[2,8,128,128]{3,2,1,0:T(8,128)(2,1)}, bf16[2,8,128,128]{3,2,1,0:T(8,128)(2,1)S(1)}, u32[]{:S(2)}, u32[]{:S(2)}) collective-permute-start(bf16[2,8,128,128]{3,2,1,0:T(8,128)(2,1)} %bitcast.31), channel_id=1, source_target_pairs={{3,0},{4,1},{5,2},{6,3},{7,4},{8,5},{9,6},{10,7},{11,8},{12,9},{13... | collective-permute-start | bytes 1572872 | tf_op jit(solution)/shard_map/ppermute | solution.py:24
  138.7 5.0 %shard_map.68.refs_2_ = f32[2,1024,256]{2,1,0:T(8,128)S(1)} custom-call(s32[1]{0:T(128)} %bitcast.35.start_ref, bf16[1024,128]{1,0:T(8,128)(2,1)S(1)} %bitcast.69, bf16[3,16,512,128]{3,2,1,0:T(8,128)(2,1)} %copy-done.19, bf16[3,2,512,128]{3,2,1,0:T(8,128)(2,1)} %collective-permute-done.9.refs_1_.refs_3_.refs_5_, bf16[3,16,512,128]{3,2,1,0:T(8,128)(2,1)} %copy-done.19, ...), custom_call_target="tpu_custom_call" | custom-call | flops 2147483648 | bytes 3670016 | tf_op jit(solution)/shard_map/pallas_call | solution.py:228
  145.0 4.8 %shard_map.66.refs_2_ = f32[2,1024,256]{2,1,0:T(8,128)S(1)} custom-call(s32[1]{0:T(128)} %bitcast.33.start_ref, bf16[1024,128]{1,0:T(8,128)(2,1)S(1)} %bitcast.70, bf16[3,16,512,128]{3,2,1,0:T(8,128)(2,1)} %copy-done.19, bf16[3,2,512,128]{3,2,1,0:T(8,128)(2,1)S(1)} %copy-done.7, bf16[3,16,512,128]{3,2,1,0:T(8,128)(2,1)} %copy-done.19, ...), custom_call_target="tpu_custom_call" | custom-call | flops 2147483648 | bytes 3670016 | tf_op jit(solution)/shard_map/pallas_call | solution.py:228
  151.2 4.9 %shard_map.64.refs_2_ = f32[2,1024,256]{2,1,0:T(8,128)S(1)} custom-call(s32[1]{0:T(128)} %bitcast.start_ref, bf16[1024,128]{1,0:T(8,128)(2,1)S(1)} %bitcast.71, bf16[3,16,512,128]{3,2,1,0:T(8,128)(2,1)} %copy-done.19, bf16[3,2,512,128]{3,2,1,0:T(8,128)(2,1)} %collective-permute-done.refs_1_.refs_3_.refs_5_, bf16[3,16,512,128]{3,2,1,0:T(8,128)(2,1)} %copy-done.19, ...), custom_call_target="tpu_custom_call" | custom-call | flops 2147483648 | bytes 3670016 | tf_op jit(solution)/shard_map/pallas_call | solution.py:228
  162.4 9.1 %shard_map.71 = (bf16[2,512,128]{2,1,0:T(8,128)(2,1)S(1)}, bf16[2,512,128]{2,1,0:T(8,128)(2,1)}) custom-call(s32[1]{0:T(128)} %bitcast.37.start_ref, bf16[2048,128]{1,0:T(8,128)(2,1)S(1)} %bitcast.64, bf16[3,16,512,128]{3,2,1,0:T(8,128)(2,1)} %copy-done.19, bf16[3,2,512,128]{3,2,1,0:T(8,128)(2,1)S(1)} %copy-done.11, f32[2,1024,256]{2,1,0:T(8,128)} %copy-done.13, ...), custom_call_target="tpu_custom_call" | custom-call | flops 4294967296 | bytes 5767168 | tf_op jit(solution)/shard_map/pallas_call | solution.py:267
  171.5 1.5 collective-permute-start.14
  173.0 9.1 %shard_map.69 = (bf16[2,512,128]{2,1,0:T(8,128)(2,1)S(1)}, bf16[2,512,128]{2,1,0:T(8,128)(2,1)}) custom-call(s32[1]{0:T(128)} %bitcast.35.start_ref, bf16[2048,128]{1,0:T(8,128)(2,1)S(1)} %bitcast.65, bf16[3,16,512,128]{3,2,1,0:T(8,128)(2,1)} %copy-done.19, bf16[3,2,512,128]{3,2,1,0:T(8,128)(2,1)} %collective-permute-done.9.refs_1_.refs_3_.refs_5_, ...), custom_call_target="tpu_custom_call" | custom-call | flops 4294967296 | bytes 5767168 | tf_op jit(solution)/shard_map/pallas_call | solution.py:267
  183.3 9.0 %shard_map.67 = (bf16[2,512,128]{2,1,0:T(8,128)(2,1)S(1)}, bf16[2,512,128]{2,1,0:T(8,128)(2,1)}) custom-call(s32[1]{0:T(128)} %bitcast.33.start_ref, bf16[2048,128]{1,0:T(8,128)(2,1)S(1)} %bitcast.66, bf16[3,16,512,128]{3,2,1,0:T(8,128)(2,1)} %copy-done.19, bf16[3,2,512,128]{3,2,1,0:T(8,128)(2,1)S(1)} %copy-done.8, f32[2,1024,256]{2,1,0:T(8,128)} %copy-done.14, ...), custom_call_target="tpu_custom_call" | custom-call | flops 4294967296 | bytes 5767168 | tf_op jit(solution)/shard_map/pallas_call | solution.py:267
  193.0 1.5 collective-permute-start.12
  194.5 9.1 %shard_map.65 = (bf16[2,512,128]{2,1,0:T(8,128)(2,1)S(1)}, bf16[2,512,128]{2,1,0:T(8,128)(2,1)}) custom-call(s32[1]{0:T(128)} %bitcast.start_ref, bf16[2048,128]{1,0:T(8,128)(2,1)S(1)} %bitcast.67, bf16[3,16,512,128]{3,2,1,0:T(8,128)(2,1)} %copy-done.19, bf16[3,2,512,128]{3,2,1,0:T(8,128)(2,1)} %collective-permute-done.refs_1_.refs_3_.refs_5_, ...), custom_call_target="tpu_custom_call" | custom-call | flops 4294967296 | bytes 5767168 | tf_op jit(solution)/shard_map/pallas_call | solution.py:267
  206.2 4.6 %collective-permute-done.11 = bf16[2,512,128]{2,1,0:T(8,128)(2,1)S(1)} collective-permute-done((bf16[2,512,128]{2,1,0:T(8,128)(2,1)}, bf16[2,512,128]{2,1,0:T(8,128)(2,1)S(1)}, u32[]{:S(2)}, u32[]{:S(2)}) %collective-permute-start.11) | collective-permute-done | bytes 262176 | tf_op jit(solution)/shard_map/ppermute | solution.py:18
  212.3 2.2 gather_fusion.3
  214.4 4.2 %fusion = bf16[512,16,128]{2,1,0:T(8,128)(2,1)} fusion(bf16[16,512,128]{2,1,0:T(8,128)(2,1)} %bitcast.81, pred[16]{0:T(512)(128)(4,1)S(1)} %broadcast_in_dim.60), kind=kLoop, calls=%fused_computation.7 | loop fusion | flops 1048576 | bytes 4194320 | tf_op jit(solution)/shard_map/transpose | solution.py:285
  (121 shorter events, 35.0 us)
Async XLA Ops:
  6.5 54.2 %copy-start = (s32[16,16,16]{2,1,0:T(8,128)S(1)}, s32[16,16,16]{2,1,0:T(8,128)}, u32[]{:S(2)}) copy-start(s32[16,16,16]{2,1,0:T(8,128)} %param.9) | copy-start | bytes 49156
  6.5 152.6 %all-gather.3.cloned.1.call-start = ((), (), s32[]{:S(2)}) async-start(), calls=%async_computation | async-start | bytes 4456448 | tf_op jit(solution)/shard_map/all_gather | solution.py:172
  10.1 2.3 %copy-start.22 = (bf16[512,16,128]{2,1,0:T(8,128)(2,1)S(1)}, bf16[512,16,128]{2,1,0:T(8,128)(2,1)}, u32[]{:S(2)}) copy-start(bf16[512,16,128]{2,1,0:T(8,128)(2,1)} %param.6) | copy-start | bytes 6291460
  10.1 2.8 %copy-start.23 = (bf16[512,16,128]{2,1,0:T(8,128)(2,1)S(1)}, bf16[512,16,128]{2,1,0:T(8,128)(2,1)}, u32[]{:S(2)}) copy-start(bf16[512,16,128]{2,1,0:T(8,128)(2,1)} %param.8) | copy-start | bytes 6291460
  17.5 2.7 %copy-start.19 = (bf16[3,16,512,128]{3,2,1,0:T(8,128)(2,1)}, bf16[3,16,512,128]{3,2,1,0:T(8,128)(2,1)S(1)}, u32[]{:S(2)}) copy-start(bf16[3,16,512,128]{3,2,1,0:T(8,128)(2,1)S(1)} %get-tuple-element.36.refs_0_.refs_2_.refs_4_) | copy-start | bytes 18874372
  23.9 13.7 %collective-permute-start.1 = (bf16[2,8,2,64,128]{4,3,1,0,2:T(8,128)(2,1)S(1)}, bf16[2,8,2,64,128]{4,3,1,0,2:T(8,128)(2,1)S(1)}, u32[]{:S(2)}, u32[]{:S(2)}) collective-permute-start(bf16[2,8,2,64,128]{4,3,1,0,2:T(8,128)(2,1)S(1)} %bitcast.90), channel_id=1, source_target_pairs={{0,16},{16,0},{1,17},{17,1},{2,18},{18,2},{3,19},{19,3},{4,20},{20... | collective-permute-start | bytes 1572872 | tf_op jit(solution)/shard_map/ppermute | solution.py:18
  40.2 19.8 %copy-start.20 = (s32[16]{0:T(128)S(1)}, s32[16]{0:T(128)}, u32[]{:S(2)}) copy-start(s32[16]{0:T(128)} %param.11) | copy-start | bytes 196
  40.3 21.2 %copy-start.25 = (s32[16]{0:T(128)S(1)}, s32[16]{0:T(128)}, u32[]{:S(2)}) copy-start(s32[16]{0:T(128)} %param.10) | copy-start | bytes 196
  43.9 31.3 %collective-permute-start.10 = (bf16[3,2,512,128]{3,2,1,0:T(8,128)(2,1)}, bf16[3,2,512,128]{3,2,1,0:T(8,128)(2,1)S(1)}, u32[]{:S(2)}, u32[]{:S(2)}) collective-permute-start(bf16[3,2,512,128]{3,2,1,0:T(8,128)(2,1)} %get-tuple-element.34), channel_id=1, source_target_pairs={{0,16},{16,0},{1,17},{17,1},{2,18},{18,2},{3,19},{19,3},{4,20},{20... | collective-permute-start | bytes 2359304 | tf_op jit(solution)/shard_map/ppermute | solution.py:18
  45.4 36.1 %collective-permute-start.9 = (bf16[3,2,512,128]{3,2,1,0:T(8,128)(2,1)}, bf16[3,2,512,128]{3,2,1,0:T(8,128)(2,1)}, u32[]{:S(2)}, u32[]{:S(2)}) collective-permute-start(bf16[3,2,512,128]{3,2,1,0:T(8,128)(2,1)} %get-tuple-element.32), channel_id=1, source_target_pairs={{0,16},{16,0},{1,17},{17,1},{2,18},{18,2},{3,19},{19,3},{4,20},{20... | collective-permute-start | bytes 2359304 | tf_op jit(solution)/shard_map/ppermute | solution.py:18
  45.9 52.4 %collective-permute-start.8 = (bf16[3,2,512,128]{3,2,1,0:T(8,128)(2,1)}, bf16[3,2,512,128]{3,2,1,0:T(8,128)(2,1)S(1)}, u32[]{:S(2)}, u32[]{:S(2)}) collective-permute-start(bf16[3,2,512,128]{3,2,1,0:T(8,128)(2,1)} %get-tuple-element.33), channel_id=1, source_target_pairs={{0,16},{16,0},{1,17},{17,1},{2,18},{18,2},{3,19},{19,3},{4,20},{20... | collective-permute-start | bytes 2359304 | tf_op jit(solution)/shard_map/ppermute | solution.py:18
  47.4 65.7 %collective-permute-start = (bf16[3,2,512,128]{3,2,1,0:T(8,128)(2,1)}, bf16[3,2,512,128]{3,2,1,0:T(8,128)(2,1)}, u32[]{:S(2)}, u32[]{:S(2)}) collective-permute-start(bf16[3,2,512,128]{3,2,1,0:T(8,128)(2,1)} %get-tuple-element.31), channel_id=1, source_target_pairs={{0,16},{16,0},{1,17},{17,1},{2,18},{18,2},{3,19},{19,3},{4,20},{20... | collective-permute-start | bytes 2359304 | tf_op jit(solution)/shard_map/ppermute | solution.py:18
  71.4 87.7 %collective-permute-start.2 = (bf16[2,8,256,128]{3,2,1,0:T(8,128)(2,1)}, bf16[2,8,256,128]{3,2,1,0:T(8,128)(2,1)S(1)}, u32[]{:S(2)}, u32[]{:S(2)}) collective-permute-start(bf16[2,8,256,128]{3,2,1,0:T(8,128)(2,1)} %bitcast.88), channel_id=1, source_target_pairs={{0,1},{1,2},{2,3},{3,4},{4,5},{5,6},{6,7},{7,8},{8,9},{9,10},{10,1... | collective-permute-start | bytes 3145736 | tf_op jit(solution)/shard_map/ppermute | solution.py:24
  76.1 83.0 %collective-permute-start.3 = (bf16[2,8,256,128]{3,2,1,0:T(8,128)(2,1)}, bf16[2,8,256,128]{3,2,1,0:T(8,128)(2,1)S(1)}, u32[]{:S(2)}, u32[]{:S(2)}) collective-permute-start(bf16[2,8,256,128]{3,2,1,0:T(8,128)(2,1)} %bitcast.89), channel_id=1, source_target_pairs={{1,0},{2,1},{3,2},{4,3},{5,4},{6,5},{7,6},{8,7},{9,8},{10,9},{11,1... | collective-permute-start | bytes 3145736 | tf_op jit(solution)/shard_map/ppermute | solution.py:24
  81.5 32.9 %collective-permute-start.4 = (bf16[2,8,128,128]{3,2,1,0:T(8,128)(2,1)}, bf16[2,8,128,128]{3,2,1,0:T(8,128)(2,1)S(1)}, u32[]{:S(2)}, u32[]{:S(2)}) collective-permute-start(bf16[2,8,128,128]{3,2,1,0:T(8,128)(2,1)} %bitcast.31), channel_id=1, source_target_pairs={{0,2},{1,3},{2,4},{3,5},{4,6},{5,7},{6,8},{7,9},{8,10},{9,11},{10,... | collective-permute-start | bytes 1572872 | tf_op jit(solution)/shard_map/ppermute | solution.py:24
  82.9 1.2 copy-start.10
  88.9 1.3 copy-start.13
  99.1 58.3 %collective-permute-start.5 = (bf16[2,8,128,128]{3,2,1,0:T(8,128)(2,1)}, bf16[2,8,128,128]{3,2,1,0:T(8,128)(2,1)S(1)}, u32[]{:S(2)}, u32[]{:S(2)}) collective-permute-start(bf16[2,8,128,128]{3,2,1,0:T(8,128)(2,1)} %bitcast.31), channel_id=1, source_target_pairs={{2,0},{3,1},{4,2},{5,3},{6,4},{7,5},{8,6},{9,7},{10,8},{11,9},{12,... | collective-permute-start | bytes 1572872 | tf_op jit(solution)/shard_map/ppermute | solution.py:24
  113.1 44.3 %collective-permute-start.6 = (bf16[2,8,128,128]{3,2,1,0:T(8,128)(2,1)}, bf16[2,8,128,128]{3,2,1,0:T(8,128)(2,1)S(1)}, u32[]{:S(2)}, u32[]{:S(2)}) collective-permute-start(bf16[2,8,128,128]{3,2,1,0:T(8,128)(2,1)} %bitcast.31), channel_id=1, source_target_pairs={{0,3},{1,4},{2,5},{3,6},{4,7},{5,8},{6,9},{7,10},{8,11},{9,12},{10... | collective-permute-start | bytes 1572872 | tf_op jit(solution)/shard_map/ppermute | solution.py:24
  114.4 43.8 %collective-permute-start.7 = (bf16[2,8,128,128]{3,2,1,0:T(8,128)(2,1)}, bf16[2,8,128,128]{3,2,1,0:T(8,128)(2,1)S(1)}, u32[]{:S(2)}, u32[]{:S(2)}) collective-permute-start(bf16[2,8,128,128]{3,2,1,0:T(8,128)(2,1)} %bitcast.31), channel_id=1, source_target_pairs={{3,0},{4,1},{5,2},{6,3},{7,4},{8,5},{9,6},{10,7},{11,8},{12,9},{13... | collective-permute-start | bytes 1572872 | tf_op jit(solution)/shard_map/ppermute | solution.py:24
  138.6 6.4 %copy-start.7 = (bf16[3,2,512,128]{3,2,1,0:T(8,128)(2,1)S(1)}, bf16[3,2,512,128]{3,2,1,0:T(8,128)(2,1)}, u32[]{:S(2)}) copy-start(bf16[3,2,512,128]{3,2,1,0:T(8,128)(2,1)} %copy-done.6) | copy-start | bytes 2359300
  143.7 1.4 copy-start.15
  149.9 1.3 copy-start.14
  156.1 1.3 copy-start.12
  159.2 1.0 copy-start.3
  161.3 1.1 copy-start.11
  171.5 11.8 %copy-start.8 = (bf16[3,2,512,128]{3,2,1,0:T(8,128)(2,1)S(1)}, bf16[3,2,512,128]{3,2,1,0:T(8,128)(2,1)}, u32[]{:S(2)}) copy-start(bf16[3,2,512,128]{3,2,1,0:T(8,128)(2,1)} %copy-done.6) | copy-start | bytes 2359300
  171.5 34.7 %collective-permute-start.14 = (bf16[2,512,128]{2,1,0:T(8,128)(2,1)}, bf16[2,512,128]{2,1,0:T(8,128)(2,1)}, u32[]{:S(2)}, u32[]{:S(2)}) collective-permute-start(bf16[2,512,128]{2,1,0:T(8,128)(2,1)} %get-tuple-element.20), channel_id=1, source_target_pairs={{0,16},{16,0},{1,17},{17,1},{2,18},{18,2},{3,19},{19,3},{4,20},{20... | collective-permute-start | bytes 786440 | tf_op jit(solution)/shard_map/ppermute | solution.py:18
  182.7 23.5 %collective-permute-start.13 = (bf16[2,512,128]{2,1,0:T(8,128)(2,1)}, bf16[2,512,128]{2,1,0:T(8,128)(2,1)}, u32[]{:S(2)}, u32[]{:S(2)}) collective-permute-start(bf16[2,512,128]{2,1,0:T(8,128)(2,1)} %get-tuple-element.19), channel_id=1, source_target_pairs={{0,16},{16,0},{1,17},{17,1},{2,18},{18,2},{3,19},{19,3},{4,20},{20... | collective-permute-start | bytes 786440 | tf_op jit(solution)/shard_map/ppermute | solution.py:18
  193.0 13.2 %collective-permute-start.12 = (bf16[2,512,128]{2,1,0:T(8,128)(2,1)}, bf16[2,512,128]{2,1,0:T(8,128)(2,1)}, u32[]{:S(2)}, u32[]{:S(2)}) collective-permute-start(bf16[2,512,128]{2,1,0:T(8,128)(2,1)} %get-tuple-element.18), channel_id=1, source_target_pairs={{0,16},{16,0},{1,17},{17,1},{2,18},{18,2},{3,19},{19,3},{4,20},{20... | collective-permute-start | bytes 786440 | tf_op jit(solution)/shard_map/ppermute | solution.py:18
  204.2 6.6 %collective-permute-start.11 = (bf16[2,512,128]{2,1,0:T(8,128)(2,1)}, bf16[2,512,128]{2,1,0:T(8,128)(2,1)S(1)}, u32[]{:S(2)}, u32[]{:S(2)}) collective-permute-start(bf16[2,512,128]{2,1,0:T(8,128)(2,1)} %get-tuple-element.17), channel_id=1, source_target_pairs={{0,16},{16,0},{1,17},{17,1},{2,18},{18,2},{3,19},{19,3},{4,20},{20... | collective-permute-start | bytes 786440 | tf_op jit(solution)/shard_map/ppermute | solution.py:18
  214.4 4.2 %copy-start.1 = (s32[16,16,16]{2,1,0:T(8,128)S(1)}, s32[16,16,16]{2,1,0:T(8,128)}, u32[]{:S(2)}) copy-start(s32[16,16,16]{2,1,0:T(8,128)} %param.9) | copy-start | bytes 49156
  (10 other events, 8.4 us)
Sparse Core Ops, SparseCore 0:
  40.3 53.6 all-gather.2

commit v2 on v1

--- a/solution.py
+++ b/solution.py
@@ -3,6 +3,7 @@
 
 import jax
 import jax.numpy as jnp
+import numpy as np
 from jax import lax
 from jax.experimental import pallas as pl
 from jax.experimental.pallas import tpu as pltpu
@@ -285,7 +286,388 @@
     return jnp.transpose(output, (1, 0, 2))
 
 
+def fused_kernel(
+    groups, tile, factor, near_slots,
+    bits_ref, mask_ref, q_ref, k_ref, v_ref, out_ref,
+    kv, kv_in, q_in, wide_in, narrow_in, anchors, state, out_away, own_bias, near_bias,
+    pair_send, pair_recv, near_send, near_recv, anchor_send, anchor_recv,
+):
+    here = lax.axis_index("head")
+    frame = lax.axis_index("frame")
+    frames = lax.axis_size("frame")
+    other = 1 - here
+    heads, rows, head_dim = q_ref.shape
+    heads_here = heads // 2
+    group_heads = heads_here // groups
+    block_rows = wide_in.shape[5]
+    part_blocks = rows // block_rows
+    own_blocks = 2 * part_blocks
+    all_rows = 2 * rows
+    column, level = frame % 4, frame // 4
+
+    def at_frame(target):
+        return {"frame": target}
+
+    level_two = (level + 2) % 4
+    level_one = level + 1 - 2 * (level % 2)
+    column_two = (column + 2) % 4
+    column_one = column + 1 - 2 * (column % 2)
+    hops = (
+        level_two * 4 + column,
+        level_one * 4 + column,
+        level * 4 + column_two,
+        level * 4 + column_one,
+    )
+    shifts = [(distance, sign) for distance in (1, 2, 3) for sign in (1, -1)]
+    neighbours = [(frame + sign * distance + frames) % frames for distance, sign in shifts]
+
+    barrier = pltpu.get_barrier_semaphore()
+    pl.semaphore_signal(
+        barrier, inc=1, device_id={"head": other}, device_id_type=pl.DeviceIdType.MESH
+    )
+    for target in list(hops) + neighbours:
+        pl.semaphore_signal(
+            barrier, inc=1, device_id=at_frame(target), device_id_type=pl.DeviceIdType.MESH
+        )
+
+    steps = part_blocks.bit_length() - 1
+    turns = [bits_ref[step] == 1 for step in range(steps)]
+
+    def turn_head(h, carry):
+        for which, ref in ((0, k_ref), (1, v_ref)):
+            blocks = [
+                ref[h, slot * block_rows : (slot + 1) * block_rows, :]
+                for slot in range(part_blocks)
+            ]
+            for step in range(steps):
+                blocks = [
+                    jnp.where(turns[step], blocks[(slot + 2**step) % part_blocks], blocks[slot])
+                    for slot in range(part_blocks)
+                ]
+            for slot in range(part_blocks):
+                place = (slot % (part_blocks // 2)) * block_rows
+                half = slot // (part_blocks // 2)
+                kv[which, h, half, place : place + block_rows, :] = blocks[slot]
+        return carry
+
+    lax.fori_loop(0, heads, turn_head, 0)
+    pl.semaphore_wait(barrier, 1 + len(hops) + len(neighbours))
+
+    def remote(src, dst, sends, recvs, index, device):
+        return pltpu.make_async_remote_copy(
+            src_ref=src,
+            dst_ref=dst,
+            send_sem=sends.at[index],
+            recv_sem=recvs.at[index],
+            device_id=device,
+            device_id_type=pl.DeviceIdType.MESH,
+        )
+
+    pair = {"head": other}
+    first = pl.ds(0, block_rows)
+    rest = pl.ds(block_rows, rows // 2 - block_rows)
+    mine = pl.ds(here * heads_here, heads_here)
+    theirs = pl.ds(other * heads_here, heads_here)
+    lead = remote(
+        kv.at[:, theirs, :, first], kv_in.at[:, :, :, first], pair_send, pair_recv, 0, pair
+    )
+    lead.start()
+
+    def near_copies(part):
+        copies = []
+        for index, (distance, sign) in enumerate(shifts):
+            if distance == 1:
+                src = kv.at[:, mine, :, first] if part == 0 else kv_in.at[:, :, :, first]
+                dst = wide_in.at[index, part]
+            else:
+                src = kv.at[:, mine, 0, first] if part == 0 else kv_in.at[:, :, 0, first]
+                dst = narrow_in.at[index - 2, part]
+            copies.append(
+                remote(
+                    src, dst, near_send, near_recv, index * 2 + part, at_frame(neighbours[index])
+                )
+            )
+        return copies
+
+    near_first, near_second = near_copies(0), near_copies(1)
+    group_copies = []
+    for group in range(groups):
+        away = pl.ds(other * heads_here + group * group_heads, group_heads)
+        land = pl.ds(group * group_heads, group_heads)
+        group_copies.append(
+            [
+                remote(
+                    kv.at[:, away, :, rest], kv_in.at[:, land, :, rest],
+                    pair_send, pair_recv, 1 + 2 * group, pair,
+                ),
+                remote(
+                    q_ref.at[away], q_in.at[land], pair_send, pair_recv, 2 + 2 * group, pair
+                ),
+            ]
+        )
+    for copy in near_first:
+        copy.start()
+    for group in range(min(2, groups)):
+        for copy in group_copies[group]:
+            copy.start()
+
+    def bias_rows(target, first_slot, count):
+        for n in range(count):
+            row = mask_ref[first_slot + n : first_slot + n + 1, :]
+            target[n * block_rows : (n + 1) * block_rows, :] = jnp.broadcast_to(
+                row, (block_rows, lanes)
+            ).astype(jnp.bfloat16)
+
+    bias_rows(own_bias, 0, own_blocks)
+    bias_rows(near_bias, own_blocks, near_slots)
+
+    lead.wait_recv()
+    for copy in near_second:
+        copy.start()
+    from_here = bits_ref[steps] == 1
+    for which in range(2):
+        for h in range(heads_here):
+            from_me = kv[which, here * heads_here + h, 0, :block_rows, :]
+            from_pair = kv_in[which, h, 0, :block_rows, :]
+            chosen = jnp.where(from_here, from_me, from_pair)
+            anchors[column // 2, column % 2, level // 2, level % 2, which, h] = chosen
+    spans = (
+        anchors.at[column // 2, column % 2, level // 2, level % 2],
+        anchors.at[column // 2, column % 2, :, level % 2],
+        anchors.at[column // 2, column % 2],
+        anchors.at[:, column % 2],
+    )
+    hop_copies = [
+        remote(spans[hop], spans[hop], anchor_send, anchor_recv, hop, at_frame(hops[hop]))
+        for hop in range(4)
+    ]
+    hop_copies[0].start()
+
+    def query_tile(h, part, start):
+        if part == 0:
+            query = q_ref[here * heads_here + h, start : start + tile, :]
+        else:
+            query = q_in[h, start : start + tile, :]
+        row = lax.broadcasted_iota(jnp.int32, (tile, lanes), 0) + (part * rows + start)
+        lane = lax.broadcasted_iota(jnp.int32, (tile, lanes), 1) * block_rows
+        inside = (row >= lane) & (row < lane + block_rows)
+        marks = jnp.where(inside, 1.0, 0.0).astype(jnp.bfloat16)
+        return jnp.concatenate([query, marks], axis=1)
+
+    tiles = [(part, start) for part in range(2) for start in range(0, rows, tile)]
+
+    def attend_own(h, carry):
+        def both(which):
+            return jnp.concatenate(
+                [
+                    kv[which, here * heads_here + h].reshape(rows, head_dim),
+                    kv_in[which, h].reshape(rows, head_dim),
+                ],
+                axis=0,
+            )
+
+        keys_marked = jnp.concatenate([both(0), own_bias[...]], axis=1)
+        value_rows = both(1)
+        values_ones = jnp.concatenate([value_rows, jnp.ones_like(value_rows)], axis=1)
+        for part, start in tiles:
+            scores = score_tile(query_tile(h, part, start), keys_marked)
+            top = jnp.max(scores, axis=1, keepdims=True)
+            weights = jnp.exp2(scores * factor - top * factor).astype(jnp.bfloat16)
+            sums = jnp.dot(weights, values_ones, preferred_element_type=jnp.float32)
+            lane = lax.broadcasted_iota(jnp.int32, (tile, head_dim), 1)
+            spot = part * rows + start
+            state[h, spot : spot + tile, :head_dim] = sums[:, :head_dim]
+            state[h, spot : spot + tile, head_dim:] = jnp.where(
+                lane < head_dim // 2, sums[:, head_dim:], top
+            )
+        return carry
+
+    def attend_near(h, carry):
+        def all_sources(which):
+            pieces = []
+            for index in range(2):
+                for part in range(2):
+                    pieces.append(wide_in[index, part, which, h].reshape(-1, head_dim))
+            for index in range(4):
+                for part in range(2):
+                    pieces.append(narrow_in[index, part, which, h])
+            for gap in range(4, frames - 3):
+                source = (frame + gap) % frames
+                pieces.append(anchors[source % 4 // 2, source % 2, source // 8, source // 4 % 2, which, h])
+            return jnp.concatenate(pieces, axis=0)
+
+        keys_marked = jnp.concatenate([all_sources(0), near_bias[...]], axis=1)
+        value_rows = all_sources(1)
+        values_ones = jnp.concatenate([value_rows, jnp.ones_like(value_rows)], axis=1)
+        for part, start in tiles:
+            scores = score_tile(query_tile(h, part, start), keys_marked)
+            spot = part * rows + start
+            own_sums = state[h, spot : spot + tile, :head_dim]
+            own_rest = state[h, spot : spot + tile, head_dim:]
+            own_total, own_top = own_rest[:, :1], own_rest[:, head_dim - 1 :]
+            top = jnp.maximum(jnp.max(scores, axis=1, keepdims=True), own_top)
+            weights = jnp.exp2(scores * factor - top * factor).astype(jnp.bfloat16)
+            sums = jnp.dot(weights, values_ones, preferred_element_type=jnp.float32)
+            shrink = jnp.exp2(own_top * factor - top * factor)
+            total = own_total * shrink + sums[:, head_dim : head_dim + 1]
+            result = (own_sums * shrink + sums[:, :head_dim]) / total
+            if part == 0:
+                out_ref[here * heads_here + h, start : start + tile, :] = result.astype(jnp.bfloat16)
+            else:
+                out_away[h, start : start + tile, :] = result.astype(jnp.bfloat16)
+        return carry
+
+    returns = []
+
+    def own_step(group):
+        for copy in group_copies[group]:
+            copy.wait_recv()
+        if group + 2 < groups:
+            for copy in group_copies[group + 2]:
+                copy.start()
+        lax.fori_loop(group * group_heads, (group + 1) * group_heads, attend_own, 0)
+
+    def near_step(group):
+        lax.fori_loop(group * group_heads, (group + 1) * group_heads, attend_near, 0)
+        copy = remote(
+            out_away.at[pl.ds(group * group_heads, group_heads)],
+            out_ref.at[pl.ds(here * heads_here + group * group_heads, group_heads)],
+            pair_send, pair_recv, 1 + 2 * groups + group, pair,
+        )
+        copy.start()
+        returns.append(copy)
+
+    own_step(0)
+    hop_copies[0].wait_recv()
+    hop_copies[1].start()
+    own_step(1)
+    hop_copies[1].wait_recv()
+    hop_copies[2].start()
+    own_step(2)
+    hop_copies[2].wait_recv()
+    hop_copies[3].start()
+    for copy in near_first + near_second:
+        copy.wait_recv()
+    hop_copies[3].wait_recv()
+    near_step(0)
+    near_step(1)
+    own_step(3)
+    near_step(2)
+    near_step(3)
+    lead.wait_send()
+    for copy in near_first + near_second + hop_copies:
+        copy.wait_send()
+    for copies in group_copies:
+        for copy in copies:
+            copy.wait_send()
+    for copy in returns:
+        copy.wait()
+
+
+def local_pair(queries, keys, values, block_mask, strides, offsets):
+    frames = lax.axis_size("frame")
+    here = lax.axis_index("head")
+    frame = lax.axis_index("frame")
+    rows, heads, head_dim = queries.shape
+    frame_blocks = block_mask.shape[1]
+    part_blocks = frame_blocks // 2
+    block_rows = rows // part_blocks
+    heads_here = heads // 2
+    groups = 4
+    wide, narrow = frame_blocks // 4, frame_blocks // 2
+    factor = head_dim ** (-0.5) * math.log2(math.e)
+
+    table = [(0, half, slot, 0) for half in range(2) for slot in range(part_blocks)]
+    for distance in (1, 2, 3):
+        for sign in (1, -1):
+            for half in range(2):
+                for slot in [0, wide] if distance == 1 else [0]:
+                    table.append((-sign * distance, half, slot, distance))
+    table += [(gap, 0, 0, frames) for gap in range(4, frames - 3)]
+    shift, half, slot, kind = (jnp.asarray(column, jnp.int32) for column in np.array(table).T)
+    near_slots = len(table) - frame_blocks
+    frame_ids = jnp.arange(frames, dtype=jnp.int32)
+
+    def looked_up(array, index):
+        return jnp.sum(jnp.where(index[:, None] == frame_ids[None, :], array[None, :], 0), axis=1)
+
+    source = lax.rem(frame + shift + frames, frames)
+    phase = looked_up(offsets, source)
+    turn = lax.rem(narrow - lax.rem(phase, narrow), narrow)
+    anchor = lax.rem(frame_blocks - lax.rem(phase, frame_blocks), frame_blocks)
+    part = jnp.where(half == 0, here, 1 - here)
+    ids = jnp.where(kind == frames, anchor, part * part_blocks + lax.rem(turn + slot, part_blocks))
+    gap = jnp.abs(frame - source)
+    spacing = jnp.where(gap == kind, looked_up(strides, gap), frame_blocks)
+    flags = (kind == 0) | (lax.rem(ids + phase, spacing) == 0)
+    steps = part_blocks.bit_length() - 1
+    powers = jnp.asarray([2**step for step in range(steps)] + [0], jnp.int32)
+    bits = jnp.where(
+        powers > 0,
+        lax.rem(turn[0] // jnp.maximum(powers, 1), 2),
+        (anchor[0] // part_blocks == here).astype(jnp.int32),
+    )
+
+    own_mask = lax.dynamic_index_in_dim(block_mask, frame, 0, keepdims=False)
+    swapped = jnp.concatenate([own_mask[part_blocks:], own_mask[:part_blocks]], axis=0)
+    own_mask = jnp.where(here == 0, own_mask, swapped)
+    block_ids = jnp.arange(frame_blocks, dtype=jnp.int32)
+    picks = ids[:, None, None] == block_ids[None, None, :]
+    kept = jnp.sum(jnp.where(picks, own_mask[None, :, :], 0), axis=2) == 1
+    mask = jnp.where(kept & flags[:, None], 0.0, masked_score).astype(jnp.float32)
+    mask = jnp.pad(mask, ((0, 0), (0, lanes - frame_blocks)))
+
+    bf16 = jnp.bfloat16
+    near_rows = near_slots * block_rows
+    all_rows = 2 * rows
+    vmem = pl.BlockSpec(memory_space=pltpu.VMEM)
+    smem = pl.BlockSpec(memory_space=pltpu.SMEM)
+    pair_count = 1 + 3 * groups
+    dma = pltpu.SemaphoreType.DMA
+    total_rows = all_rows + near_rows
+    output = pl.pallas_call(
+        functools.partial(fused_kernel, groups, min(256, rows), factor, near_slots),
+        out_shape=jax.ShapeDtypeStruct((heads, rows, head_dim), bf16),
+        in_specs=[smem, vmem, vmem, vmem, vmem],
+        out_specs=vmem,
+        scratch_shapes=[
+            pltpu.VMEM((2, heads, 2, rows // 2, head_dim), bf16),
+            pltpu.VMEM((2, heads_here, 2, rows // 2, head_dim), bf16),
+            pltpu.VMEM((heads_here, rows, head_dim), bf16),
+            pltpu.VMEM((2, 2, 2, heads_here, 2, block_rows, head_dim), bf16),
+            pltpu.VMEM((4, 2, 2, heads_here, block_rows, head_dim), bf16),
+            pltpu.VMEM((2, 2, 2, 2, 2, heads_here, block_rows, head_dim), bf16),
+            pltpu.VMEM((heads_here, all_rows, 2 * head_dim), jnp.float32),
+            pltpu.VMEM((heads_here, rows, head_dim), bf16),
+            pltpu.VMEM((all_rows, lanes), bf16),
+            pltpu.VMEM((near_rows, lanes), bf16),
+            dma((pair_count,)),
+            dma((pair_count,)),
+            dma((12,)),
+            dma((12,)),
+            dma((4,)),
+            dma((4,)),
+        ],
+        compiler_params=pltpu.CompilerParams(
+            collective_id=0, has_side_effects=True, vmem_limit_bytes=56 * 1024 * 1024
+        ),
+        cost_estimate=pl.CostEstimate(
+            flops=heads_here * 8 * all_rows * total_rows * head_dim,
+            bytes_accessed=8 * heads * rows * head_dim,
+            transcendentals=heads_here * all_rows * total_rows,
+        ),
+    )(
+        bits,
+        mask,
+        jnp.transpose(queries, (1, 0, 2)),
+        jnp.transpose(keys, (1, 0, 2)),
+        jnp.transpose(values, (1, 0, 2)),
+    )
+    return jnp.transpose(output, (1, 0, 2))
+
+
 def solution(mesh):
+    paired = mesh.shape["head"] == 2 and mesh.shape["frame"] == 16
     placed = (
         P(("frame", "head"), None, None),
         P(("frame", "head"), None, None),
@@ -295,7 +677,7 @@
         P(),
     )
     return jax.shard_map(
-        local,
+        local_pair if paired else local,
         mesh=mesh,
         in_specs=placed,
         out_specs=P(("frame", "head"), None, None),

time: 226 us -> 147 us (0.65)
  the two profiles are of different devices: /device:TPU:26 before, /device:TPU:0 now
where the time goes in v2:
time: 147 us
  Pallas kernels  130 us (88%)
  local copies, waits for them, and re-layouts  12.4 us (8%)
  other arithmetic  4.6 us (3%)
    pallas_call x1, Pallas kernels, local_pair(): pl.pallas_call(functools.partial(fused_kernel, groups, min(256, rows), fa...  130 us
    transpose x1, local copies, waits for them, and re-layouts, local_pair(): return jnp.transpose(output, (1, 0, 2))  4.26 us
    unnamed x5, local copies, waits for them, and re-layouts  3.61 us
    transpose x1, local copies, waits for them, and re-layouts, local_pair(): jnp.transpose(values, (1, 0, 2))  3.17 us

profile of v2, /device:TPU:0, one launch (start us, length us, event | category | flops | bytes accessed | tf_op | source)
XLA Modules:
  0.0 147.1 jit_solution(4487788519008683547)
XLA Ops:
  0.0 0.7 subtract_abs_fusion
  0.7 0.8 select_reduce_fusion.1
  1.4 0.9 compare_or_fusion
  2.5 1.4 fusion.5.bits_ref
  3.9 0.7 constant_dynamic-slice_fusion
  4.6 0.7 fusion
  5.3 0.1 select_reduce_fusion
  5.4 0.1 copy.16
  5.5 0.1 and_select_fusion
  5.6 0.6 pad.4.mask_ref
  6.2 0.0 copy-start
  6.2 0.0 copy-start.1
  6.2 3.6 %copy.24 = bf16[512,16,128]{2,0,1:T(8,128)(2,1)} copy(bf16[512,16,128]{2,1,0:T(8,128)(2,1)} %param.11) | data formatting | bytes 4194304 | tf_op args[0]
  9.8 0.0 copy-done
  9.8 0.0 copy-done.1
  9.8 3.2 %copy_bitcast_fusion = (bf16[16,512,128]{2,1,0:T(8,128)(2,1)}, bf16[16,512,128]{2,1,0:T(8,128)(2,1)}) fusion(bf16[512,16,128]{2,1,0:T(8,128)(2,1)S(1)} %copy-done, bf16[512,16,128]{2,1,0:T(8,128)(2,1)S(1)} %copy-done.1), kind=kLoop, calls=%fused_computation | loop fusion | bytes 8388608 | tf_op jit(solution)/shard_map/transpose | solution.py:664
  13.0 129.8 %shard_map.109 = bf16[16,512,128]{2,1,0:T(8,128)(2,1)} custom-call(s32[4]{0:T(128)} %fusion.5.bits_ref, f32[41,128]{1,0:T(8,128)} %pad.4.mask_ref, bf16[16,512,128]{2,1,0:T(8,128)(2,1)} %bitcast.14, bf16[16,512,128]{2,1,0:T(8,128)(2,1)} %get-tuple-element.16.k_ref, bf16[16,512,128]{2,1,0:T(8,128)(2,1)} %get-tuple-element.15.v_ref), custom_call_target="tpu_custom_call" | custom-call | flops 22011707392 | bytes 8388608 | tf_op jit(solution)/shard_map/pallas_call | solution.py:628
  142.8 4.3 %copy.20 = bf16[512,16,128]{2,1,0:T(8,128)(2,1)} copy(bf16[512,16,128]{2,0,1:T(8,128)(2,1)} %bitcast.15) | data formatting | bytes 4194304 | tf_op jit(solution)/shard_map/transpose | solution.py:666
  (1 shorter events, 0.0 us)
Async XLA Ops:
  6.2 3.6 %copy-start = (bf16[512,16,128]{2,1,0:T(8,128)(2,1)S(1)}, bf16[512,16,128]{2,1,0:T(8,128)(2,1)}, u32[]{:S(2)}) copy-start(bf16[512,16,128]{2,1,0:T(8,128)(2,1)} %param.13) | copy-start | bytes 6291460
  6.2 3.6 %copy-start.1 = (bf16[512,16,128]{2,1,0:T(8,128)(2,1)S(1)}, bf16[512,16,128]{2,1,0:T(8,128)(2,1)}, u32[]{:S(2)}) copy-start(bf16[512,16,128]{2,1,0:T(8,128)(2,1)} %param.12) | copy-start | bytes 6291460

commit v3 on v2

--- a/solution.py
+++ b/solution.py
@@ -537,15 +537,10 @@
         copy.start()
         returns.append(copy)
 
-    own_step(0)
-    hop_copies[0].wait_recv()
-    hop_copies[1].start()
-    own_step(1)
-    hop_copies[1].wait_recv()
-    hop_copies[2].start()
-    own_step(2)
-    hop_copies[2].wait_recv()
-    hop_copies[3].start()
+    for group in range(3):
+        hop_copies[group].wait_recv()
+        hop_copies[group + 1].start()
+        own_step(group)
     for copy in near_first + near_second:
         copy.wait_recv()
     hop_copies[3].wait_recv()

time: 147 us -> 149 us (1.014)
  Pallas kernels: 130 us -> 132 us
    pallas_call x1, Pallas kernels: 130 us -> 132 us  [local_pair(): pl.pallas_call(functools.partial(fused_kernel, groups, min(256, rows), fa...]
where the time goes in v3:
time: 149 us
  Pallas kernels  132 us (89%)
  local copies, waits for them, and re-layouts  12.4 us (8%)
  other arithmetic  4.6 us (3%)
    pallas_call x1, Pallas kernels, local_pair(): pl.pallas_call(functools.partial(fused_kernel, groups, min(256, rows), fa...  132 us
    transpose x1, local copies, waits for them, and re-layouts, local_pair(): return jnp.transpose(output, (1, 0, 2))  4.26 us
    unnamed x5, local copies, waits for them, and re-layouts  3.61 us
    transpose x1, local copies, waits for them, and re-layouts, local_pair(): jnp.transpose(values, (1, 0, 2))  3.17 us

profile of v3, /device:TPU:0, one launch (start us, length us, event | category | flops | bytes accessed | tf_op | source)
XLA Modules:
  0.0 148.9 jit_solution(3742966406623757508)
XLA Ops:
  0.0 0.7 subtract_abs_fusion
  0.7 0.8 select_reduce_fusion.1
  1.4 0.9 compare_or_fusion
  2.5 1.4 fusion.5.bits_ref
  3.9 0.7 constant_dynamic-slice_fusion
  4.6 0.7 fusion
  5.3 0.1 select_reduce_fusion
  5.4 0.1 copy.16
  5.5 0.1 and_select_fusion
  5.6 0.6 pad.4.mask_ref
  6.2 0.0 copy-start
  6.2 0.0 copy-start.1
  6.2 3.6 %copy.24 = bf16[512,16,128]{2,0,1:T(8,128)(2,1)} copy(bf16[512,16,128]{2,1,0:T(8,128)(2,1)} %param.11) | data formatting | bytes 4194304 | tf_op args[0]
  9.8 0.0 copy-done
  9.8 0.0 copy-done.1
  9.8 3.2 %copy_bitcast_fusion = (bf16[16,512,128]{2,1,0:T(8,128)(2,1)}, bf16[16,512,128]{2,1,0:T(8,128)(2,1)}) fusion(bf16[512,16,128]{2,1,0:T(8,128)(2,1)S(1)} %copy-done, bf16[512,16,128]{2,1,0:T(8,128)(2,1)S(1)} %copy-done.1), kind=kLoop, calls=%fused_computation | loop fusion | bytes 8388608 | tf_op jit(solution)/shard_map/transpose | solution.py:659
  13.0 131.7 %shard_map.109 = bf16[16,512,128]{2,1,0:T(8,128)(2,1)} custom-call(s32[4]{0:T(128)} %fusion.5.bits_ref, f32[41,128]{1,0:T(8,128)} %pad.4.mask_ref, bf16[16,512,128]{2,1,0:T(8,128)(2,1)} %bitcast.14, bf16[16,512,128]{2,1,0:T(8,128)(2,1)} %get-tuple-element.16.k_ref, bf16[16,512,128]{2,1,0:T(8,128)(2,1)} %get-tuple-element.15.v_ref), custom_call_target="tpu_custom_call" | custom-call | flops 22011707392 | bytes 8388608 | tf_op jit(solution)/shard_map/pallas_call | solution.py:623
  144.7 4.3 %copy.20 = bf16[512,16,128]{2,1,0:T(8,128)(2,1)} copy(bf16[512,16,128]{2,0,1:T(8,128)(2,1)} %bitcast.15) | data formatting | bytes 4194304 | tf_op jit(solution)/shard_map/transpose | solution.py:661
  (1 shorter events, 0.0 us)
Async XLA Ops:
  6.2 3.6 %copy-start = (bf16[512,16,128]{2,1,0:T(8,128)(2,1)S(1)}, bf16[512,16,128]{2,1,0:T(8,128)(2,1)}, u32[]{:S(2)}) copy-start(bf16[512,16,128]{2,1,0:T(8,128)(2,1)} %param.13) | copy-start | bytes 6291460
  6.2 3.6 %copy-start.1 = (bf16[512,16,128]{2,1,0:T(8,128)(2,1)S(1)}, bf16[512,16,128]{2,1,0:T(8,128)(2,1)}, u32[]{:S(2)}) copy-start(bf16[512,16,128]{2,1,0:T(8,128)(2,1)} %param.12) | copy-start | bytes 6291460
